TPU v7x, 512 devices: a whole 4x8x8 slice. The times are simulated.
512 devices in a mesh: section: 16 (over y, x_hi), dp: 32 (over z, x_lo, core).
Axes of the slice: x: 4 (x_hi: 2, x_lo: 2; x = x_hi * 2 + x_lo), y: 8, z: 8, core: 2. Of those that a mesh axis runs over, the one named last changes fastest.
Arguments:
- saved_states: bfloat16 [16, 2, 128, 2688], P('section', None, 'dp'), may hold values from -64 to 64
- cotangent_in: bfloat16 [16, 128, 2688], P('section', 'dp'), may hold values from -6 to 6
- lengths: int32 [16], P('section'), may hold values from 16 to 128
- gain: bfloat16 [2688], replicated, may hold values from 0.099609375 to 1.8984375
- up_weight: bfloat16 [2688, 9216], P('section', 'dp'), may hold values from -0.125 to 0.125
- down_weight: bfloat16 [9216, 2688], P('dp', 'section'), may hold values from -0.0625 to 0.0625
Outputs:
- cotangent_out: bfloat16 [16, 128, 2688], P('section', 'dp')
- up_gradient: bfloat16 [2688, 9216], P('section', 'dp')
- down_gradient: bfloat16 [9216, 2688], P('dp', 'section')
- gain_gradient: float32 [2688], replicated
All inputs are finite; a program needn't handle non-finite values.
Results may differ from a plain program's by a relative error of at most 0.024.
Values may be sent and summed in bfloat16 or wider, within the bound.
A program may use at most 64 MiB of HBM per device.

v0:
```python
import math

import jax
import jax.numpy as jnp
from jax import lax
from jax.sharding import PartitionSpec as P

epsilon = 1e-06


def passed_along(block, axis, distance):
    devices = range(lax.axis_size(axis))
    route = [((i - distance) % len(devices), i) for i in devices]
    return lax.ppermute(block, axis, route)


def back_iteration(state, cotangent, gain, up_full, down_full):
    values = state.astype(jnp.float32)
    reciprocal = lax.rsqrt(jnp.mean(values * values, axis=-1, keepdims=True) + epsilon)
    scaled = values * reciprocal
    gain_wide = gain.astype(jnp.float32)
    normed = (scaled * gain_wide).astype(jnp.bfloat16)
    hidden_in = jnp.dot(normed, up_full, preferred_element_type=jnp.float32)
    sigma = jax.nn.sigmoid(hidden_in)
    hidden_out = (hidden_in * sigma).astype(jnp.bfloat16)
    back_out = lax.dot_general(
        cotangent, down_full, (((1,), (1,)), ((), ())), preferred_element_type=jnp.float32
    )
    back_in = (back_out * sigma * (1.0 + hidden_in * (1.0 - sigma))).astype(jnp.bfloat16)
    partial_value = lax.dot_general(
        back_in, up_full, (((1,), (1,)), ((), ())), preferred_element_type=jnp.float32
    )
    back_normed = lax.psum(partial_value.astype(jnp.bfloat16), "dp").astype(jnp.float32)
    rows_scaled, rows_recip, rows_cot = (scaled, reciprocal, cotangent)
    gained = back_normed * gain_wide
    back_state = rows_recip * (
        gained - rows_scaled * jnp.mean(gained * rows_scaled, axis=-1, keepdims=True)
    )
    result = (rows_cot.astype(jnp.float32) + back_state).astype(jnp.bfloat16)
    gain_term = jnp.sum(back_normed * rows_scaled, axis=0)
    return (result, normed, back_in, hidden_out, gain_term)


def hand_over(result):
    moved = passed_along(result, "section", -1)
    return moved


def contract_rows(left, right):
    return lax.dot_general(
        left, right, (((0,), (0,)), ((), ())), preferred_element_type=jnp.float32
    )


def reduce_terms(up_terms, down_terms):
    return (
        lax.psum_scatter(
            up_terms.astype(jnp.bfloat16), "section", scatter_dimension=0, tiled=True
        ).astype(jnp.float32),
        lax.psum_scatter(
            down_terms.astype(jnp.bfloat16), "section", scatter_dimension=1, tiled=True
        ).astype(jnp.float32),
    )


def on_device(saved_states, cotangent_in, lengths, gain, up_weight, down_weight):
    up_full, down_full = (
        lax.all_gather(up_weight, "section", axis=0, tiled=True),
        lax.all_gather(down_weight, "section", axis=1, tiled=True),
    )
    group_states, group_cotangent = (
        lax.all_gather(saved_states, "dp", axis=2, tiled=True),
        lax.all_gather(cotangent_in, "dp", axis=1, tiled=True),
    )
    turns = group_states.shape[1]
    tokens = group_states.shape[2]
    share = saved_states.shape[2]
    member = lax.axis_index("dp")
    positions = lax.broadcasted_iota(jnp.int32, (tokens, 1), 0)
    cotangent = jnp.where(
        positions < lengths[0], group_cotangent[0], jnp.zeros_like(group_cotangent[0])
    )
    scale = 1.0 / math.sqrt(turns * tokens * lax.axis_size("section"))
    gain_total = jnp.zeros((gain.shape[0],), jnp.float32)
    up_total = jnp.zeros(up_full.shape, jnp.float32)
    down_total = jnp.zeros(down_full.shape, jnp.float32)
    result = cotangent
    for turn in range(turns):
        if turn > 0:
            cotangent = hand_over(result)
        result, normed, back_in, hidden_out, gain_term = back_iteration(
            group_states[0, turn], cotangent, gain, up_full, down_full
        )
        gain_total = gain_total + gain_term
        up_total = up_total + contract_rows(normed, back_in)
        down_total = down_total + contract_rows(hidden_out, cotangent)
    up_sum, down_sum = reduce_terms(up_total * scale, down_total * scale)
    gain_sum = lax.psum(gain_total * scale, "section")
    own_rows = lax.dynamic_slice_in_dim(result, member * share, share, 0)[None]
    return (own_rows, up_sum.astype(jnp.bfloat16), down_sum.astype(jnp.bfloat16), gain_sum)


def solution(mesh):
    placed = (
        P("section", None, "dp", None),
        P("section", "dp", None),
        P("section"),
        P(),
        P("section", "dp"),
        P("dp", "section"),
    )
    return jax.shard_map(
        on_device,
        mesh=mesh,
        in_specs=placed,
        out_specs=(P("section", "dp", None), P("section", "dp"), P("dp", "section"), P()),
        check_vma=False,
    )
```

profile of v0, /device:TPU:6, one launch (start us, length us, event | category | flops | bytes accessed | tf_op | source)
XLA Modules:
  0.0 1155.2 jit_solution(15592596476500519794)
XLA Ops:
  7.2 1.4 copy.15
  12.3 44.2 %all_gather.12 = bf16[1,128,2688]{2,0,1:T(2,128)(2,1)} all-gather(bf16[1,4,2688]{2,0,1:T(2,128)(2,1)S(1)} %copy.14), channel_id=1, replica_groups=mesh['section'=16,'dp'=32] {'dp'}, dimensions={1}, use_global_device_ids=true | all-gather | bytes 709632 | tf_op jit(solution)/shard_map/all_gather | solution.py:73
  56.5 25.5 %all-gather.4.cloned.1.call-done = bf16[1,2,128,2688]{3,1,0,2:T(2,128)(2,1)} async-done(((bf16[1,2,4,2688]{3,1,0,2:T(2,128)(2,1)}), bf16[1,2,128,2688]{3,1,0,2:T(2,128)(2,1)}) %all-gather.4.cloned.1.call-update) | async-done | bytes 1376272 | tf_op jit(solution)/shard_map/all_gather | solution.py:72
  82.1 5.2 fusion.36
  87.6 86.6 %all-gather.8.cloned.1.call-done = bf16[2688,288]{1,0:T(8,128)(2,1)} async-done(((bf16[168,288]{1,0:T(8,128)(2,1)}), bf16[2688,288]{1,0:T(8,128)(2,1)}) %all-gather.8.cloned.1.call-update) | async-done | bytes 1548304 | tf_op jit(solution)/shard_map/all_gather | solution.py:68
  174.2 2.4 fusion.25
  176.6 88.4 %all-gather.6.cloned.1.call-done = bf16[288,2688]{0,1:T(8,128)(2,1)} async-done(((bf16[288,168]{0,1:T(8,128)(2,1)}), bf16[288,2688]{0,1:T(8,128)(2,1)}) %all-gather.6.cloned.1.call-update) | async-done | bytes 1548304 | tf_op jit(solution)/shard_map/all_gather | solution.py:69
  265.0 2.9 fusion.20
  267.9 1.6 convolution_convert_fusion.1
  269.6 225.1 %all-reduce.5.cloned.1.call-done = bf16[128,2688]{1,0:T(8,128)(2,1)} async-done(((bf16[128,2688]{1,0:T(8,128)(2,1)}), bf16[128,2688]{1,0:T(8,128)(2,1)}) %all-reduce.5.cloned.1.call-update) | async-done | bytes 688144 | tf_op jit(solution)/shard_map/psum | solution.py:33
  494.7 1.7 fusion.15
  496.5 1.7 fusion.11
  498.2 4.0 collective-permute-start
  503.4 13.4 %collective-permute-done = bf16[128,2688]{1,0:T(8,128)(2,1)S(1)} collective-permute-done((bf16[128,2688]{1,0:T(8,128)(2,1)S(1)}, bf16[128,2688]{1,0:T(8,128)(2,1)S(1)}, u32[]{:S(2)}, u32[]{:S(2)}) %collective-permute-start) | collective-permute-done | bytes 688160 | tf_op jit(solution)/shard_map/ppermute | solution.py:14
  517.6 1.7 convolution_convert_fusion
  519.4 1.7 fusion.23
  521.1 2.2 fusion.2
  525.4 2.1 fusion.3
  527.6 220.0 %all-reduce.7.cloned.1.call-done = bf16[128,2688]{1,0:T(8,128)(2,1)} async-done(((bf16[128,2688]{1,0:T(8,128)(2,1)}), bf16[128,2688]{1,0:T(8,128)(2,1)}) %all-reduce.7.cloned.1.call-update) | async-done | bytes 688144 | tf_op jit(solution)/shard_map/psum | solution.py:33
  747.6 2.5 fusion.12
  750.2 71.8 %psum.23 = f32[2688]{0:T(1024)} all-reduce(f32[2688]{0:T(1024)S(1)} %add_multiply_fusion), channel_id=1, replica_groups=mesh['section'=16,'dp'=32] {'section'}, use_global_device_ids=true, to_apply=%region_10.11 | all-reduce | flops 2688 | bytes 21504 | tf_op jit(solution)/shard_map/psum | solution.py:98
  822.1 1.6 fusion.33
  823.6 125.2 %reduce-scatter.7.cloned.1.call-done = bf16[168,288]{1,0:T(8,128)(2,1)} async-done(((bf16[2688,288]{1,0:T(8,128)(2,1)}), bf16[168,288]{1,0:T(8,128)(2,1)}) %reduce-scatter.7.cloned.1.call-update) | async-done | bytes 96784
  948.8 199.6 %reduce-scatter.9.cloned.1.call-done = bf16[288,168]{0,1:T(8,128)(2,1)} async-done(((bf16[288,2688]{0,1:T(8,128)(2,1)}), bf16[288,168]{0,1:T(8,128)(2,1)}) %reduce-scatter.9.cloned.1.call-update) | async-done | bytes 96784
  (53 shorter events, 7.7 us)
Async XLA Ops:
  7.2 74.9 %all-gather.4.cloned.1.call-start = ((), (), s32[]{:S(2)}) async-start(), calls=%async_computation.2 | async-start | bytes 1419264 | tf_op jit(solution)/shard_map/all_gather | solution.py:72
  8.7 165.5 %all-gather.8.cloned.1.call-start = ((), (), s32[]{:S(2)}) async-start(), calls=%async_computation.4 | async-start | bytes 2193408 | tf_op jit(solution)/shard_map/all_gather | solution.py:68
  9.4 255.6 %all-gather.6.cloned.1.call-start = ((), (), s32[]{:S(2)}) async-start(), calls=%async_computation.3 | async-start | bytes 2193408 | tf_op jit(solution)/shard_map/all_gather | solution.py:69
  10.2 484.5 %all-reduce.5.cloned.1.call-start = ((), (), s32[]{:S(2)}) async-start(), calls=%async_computation.5 | async-start | bytes 1376256 | tf_op jit(solution)/shard_map/psum | solution.py:33
  176.6 91.3 %copy-start.9 = (f32[128,288]{0,1:T(8,128)}, f32[128,288]{0,1:T(8,128)S(1)}, u32[]{:S(2)}) copy-start(f32[128,288]{0,1:T(8,128)S(1)} %fusion.25) | copy-start | bytes 442372
  176.6 91.3 %copy-start = (bf16[2688,288]{1,0:T(8,128)(2,1)S(1)}, bf16[2688,288]{1,0:T(8,128)(2,1)}, u32[]{:S(2)}) copy-start(bf16[2688,288]{1,0:T(8,128)(2,1)} %all-gather.8.cloned.1.call-done) | copy-start | bytes 4644868
  267.9 1.7 copy-start.11
  269.6 478.0 %all-reduce.7.cloned.1.call-start = ((), (), s32[]{:S(2)}) async-start(), calls=%async_computation.6 | async-start | bytes 1376256 | tf_op jit(solution)/shard_map/psum | solution.py:33
  494.7 1.8 copy-start.1
  496.5 5.8 copy-start.3
  498.2 18.5 %collective-permute-start = (bf16[128,2688]{1,0:T(8,128)(2,1)S(1)}, bf16[128,2688]{1,0:T(8,128)(2,1)S(1)}, u32[]{:S(2)}, u32[]{:S(2)}) collective-permute-start(bf16[128,2688]{1,0:T(8,128)(2,1)S(1)} %fusion.11), channel_id=1, source_target_pairs={{32,0},{64,32},{96,64},{128,96},{160,128},{192,160},{224,192},{256... | collective-permute-start | bytes 2064392 | tf_op jit(solution)/shard_map/ppermute | solution.py:14
  502.5 14.2 %copy-start.8 = (bf16[288,2688]{0,1:T(8,128)(2,1)S(1)}, bf16[288,2688]{0,1:T(8,128)(2,1)}, u32[]{:S(2)}) copy-start(bf16[288,2688]{0,1:T(8,128)(2,1)} %all-gather.6.cloned.1.call-done) | copy-start | bytes 4644868
  503.4 14.2 %copy-start.6 = (f32[128,288]{0,1:T(8,128)}, f32[128,288]{0,1:T(8,128)S(1)}, u32[]{:S(2)}) copy-start(f32[128,288]{0,1:T(8,128)S(1)} %fusion.22) | copy-start | bytes 442372
  516.7 0.9 copy-start.4
  519.3 429.5 %reduce-scatter.7.cloned.1.call-start = ((), (), s32[]{:S(2)}) async-start(), calls=%async_computation.7 | async-start | bytes 2193408
  523.2 1.3 copy-start.2
  523.2 1.3 copy-start.10
  523.2 2.1 copy-start.5
  523.3 2.1 copy-start.7
  523.3 625.1 %reduce-scatter.9.cloned.1.call-start = ((), (), s32[]{:S(2)}) async-start(), calls=%async_computation.8 | async-start | bytes 2193408
Sparse Core Ops, SparseCore 0:
  10.7 71.3 all-gather.3
  85.3 88.8 all-gather.7
  177.4 87.6 all-gather.5
  269.7 224.9 all-reduce.4
  519.4 228.1 all-reduce.6
  752.6 196.1 reduce-scatter.6
  953.9 194.4 reduce-scatter.8
where the time goes:
time: 1160 us
  waiting for transfers between devices  985 us (85%)
  blocking collectives  116 us (10%)
  matrix products  17 us (1%)
  between operations  15 us (1%)
    psum x2, waiting for transfers between devices, back_iteration(): lax.psum(partial_value.astype(jnp.bfloat16), 'dp').astype(jnp.float32)  445 us
    unnamed x9, waiting for transfers between devices  326 us
    all_gather x1, waiting for transfers between devices, on_device(): lax.all_gather(down_weight, 'section', axis=1, tiled=True)  88.4 us
    all_gather x1, waiting for transfers between devices, on_device(): lax.all_gather(up_weight, 'section', axis=0, tiled=True)  86.6 us
    psum x1, blocking collectives, on_device(): gain_sum = lax.psum(gain_total * scale, 'section')  71.8 us
    all_gather x1, blocking collectives, on_device(): lax.all_gather(cotangent_in, 'dp', axis=1, tiled=True)  44.2 us
    all_gather x1, waiting for transfers between devices, on_device(): lax.all_gather(saved_states, 'dp', axis=2, tiled=True)  25.5 us
  transfers between devices with their start and end apart: 8, of which 8 were waited for; matrix products, arithmetic and copies ran while one was open for 2% of the time, Pallas kernels for 0%

commit v1 on v0

v1 whole, which is shorter than its diff:
```python
import functools
import math

import jax
import jax.numpy as jnp
from jax import lax
from jax.experimental import pallas as pl
from jax.experimental.pallas import tpu as pltpu
from jax.sharding import PartitionSpec as P

MESH = pl.DeviceIdType.MESH
F32, BF16 = jnp.float32, jnp.bfloat16
epsilon = 1e-06

Y_ITEMS = {
    1: ((0, 0), (1, 0), (0, 1), (1, 1), (0, 2), (1, 2), (0, 3)),
    -1: ((0, 0), (1, 0), (0, 1), (1, 1), (0, 2), (1, 2), (1, 3)),
}
G_ITEMS = {
    1: ((0, 4), (1, 3), (0, 3), (1, 2), (0, 2), (1, 1), (0, 1)),
    -1: ((1, 4), (0, 3), (1, 3), (0, 2), (1, 2), (0, 1), (1, 1)),
}
Z_REACH = {1: 4, -1: 3}
DIRS = (1, -1)


def mod(a, n):
    return lax.rem(a + n, n)


def dot(a, b):
    return jnp.dot(a, b, preferred_element_type=F32)


def dot_t(a, b):
    return lax.dot_general(a, b, (((1,), (1,)), ((), ())), preferred_element_type=F32)


def kernel(
    scale, states, cot_in, lengths, gain, up, down,
    cot_out, up_out, down_out, gain_out,
    w, e_s, e_c, acts, cots, xn, xc, bm, hm, br, hr,
    pb, rc, qb, rz, st, sr, res, gs, gr, fs, fr,
    ga, gz, gy, send, recv,
):
    s, p = lax.axis_index("section"), lax.axis_index("dp")
    y, h = lax.div(s, 2), lax.rem(s, 2)
    z, l, c = lax.div(p, 4), lax.rem(lax.div(p, 2), 2), lax.rem(p, 2)
    g = 1 - h

    def at(section=None, dp=None):
        return {"section": s if section is None else section, "dp": p if dp is None else dp}

    def at_y(k):
        return at(section=mod(y + k, 8) * 2 + h)

    def at_z(k):
        return at(dp=mod(z + k, 8) * 4 + l * 2 + c)

    pair_h = at(section=s + 1 - 2 * h)
    pair_l = at(dp=p + 2 - 4 * l)
    pair_c = at(dp=p + 1 - 2 * c)
    before = at(section=mod(s - 1, 16))
    cross = at(section=mod(s - 1 + 2 * h, 16))

    count = [0]

    class Copy:
        def __init__(self, src, dst, landing, device):
            k = count[0]
            count[0] += 1
            self.out = pltpu.make_async_remote_copy(
                src_ref=src, dst_ref=dst, send_sem=send.at[k], recv_sem=recv.at[k],
                device_id=device, device_id_type=MESH,
            )
            self.arrival = pltpu.make_async_remote_copy(
                src_ref=src, dst_ref=landing, send_sem=send.at[k], recv_sem=recv.at[k],
                device_id=device, device_id_type=MESH,
            )
            pending.append(self)
            self.out.start()

        def arrived(self):
            self.arrival.wait_recv()

    pending = []

    barrier = pltpu.get_barrier_semaphore()
    partners = [at_y(k) for k in range(1, 8)] + [at_z(k) for k in range(1, 8)]
    partners += [pair_h, pair_l, pair_c, cross]
    for device in partners:
        pl.semaphore_signal(barrier, inc=1, device_id=device, device_id_type=MESH)

    down_t = down[...].astype(F32).T
    up_own = up[...].astype(F32)
    rows = up_own.shape[0]
    w[y, h, :, 0:256] = up_own[:, 0:256].astype(BF16)
    w[y, h, :, 256:512] = down_t[:, 0:256].astype(BF16)
    w[y, h, :, 512:640] = jnp.concatenate(
        [up_own[:, 256:288], down_t[:, 256:288], jnp.zeros((rows, 64), F32)], axis=1
    ).astype(BF16)
    e_s[l] = states[0]
    e_c[l] = cot_in[0]

    pl.semaphore_wait(barrier, len(partners))

    swap_s = Copy(e_s.at[l], e_s.at[l], e_s.at[1 - l], pair_l)
    swap_c = Copy(e_c.at[l], e_c.at[l], e_c.at[1 - l], pair_l)
    swap_w = Copy(w.at[y, h], w.at[y, h], w.at[y, g], pair_h)

    y_copies = {}

    def y_step(i):
        for way in DIRS:
            sub, far = Y_ITEMS[way][i]
            if far > 0:
                y_copies[way, sub, far - 1].arrived()
            elif sub == 1 and way == 1:
                swap_w.arrived()
            row = mod(y - way * far, 8)
            land = mod(y - way * (far + 1), 8)
            at_h = g if sub else h
            y_copies[way, sub, far] = Copy(w.at[row, at_h], w.at[row, at_h], w.at[land, at_h], at_y(way))

    y_step(0)

    gain_wide = gain[...].astype(F32)
    swap_s.arrived()
    swap_c.arrived()
    in_chunk = lax.broadcasted_iota(jnp.int32, (8, 1), 0)
    position = z * 16 + c * 4 + jnp.where(in_chunk >= 4, in_chunk + 4, in_chunk)
    d = gain_wide.shape[1]

    def own_state(m):
        values = jnp.concatenate([e_s[0, m].astype(F32), e_s[1, m].astype(F32)], axis=0)
        reciprocal = lax.rsqrt(jnp.mean(values * values, axis=-1, keepdims=True) + epsilon)
        return values * reciprocal, reciprocal

    for m in range(2):
        acts[m, z, c] = (own_state(m)[0] * gain_wide).astype(BF16)
    raw = jnp.concatenate([e_c[0].astype(F32), e_c[1].astype(F32)], axis=0)
    acts[2, z, c] = jnp.where(position < lengths[0], raw, 0.0).astype(BF16)

    z_copies, c_copies = {}, []

    def to_core(row):
        c_copies.append(
            Copy(acts.at[:, row, c], acts.at[:, row, c], acts.at[:, row, 1 - c], pair_c)
        )

    def z_step(far):
        if far == 0:
            to_core(z)
        for way in DIRS:
            if far > Z_REACH[way]:
                continue
            row = mod(z - way * far, 8)
            if far > 0:
                z_copies[way, far - 1].arrived()
            if far < Z_REACH[way]:
                land = mod(z - way * (far + 1), 8)
                z_copies[way, far] = Copy(
                    acts.at[:, row, c], acts.at[:, row, c], acts.at[:, land, c], at_z(way)
                )
            if far > 0:
                to_core(row)

    def turned(value):
        return value.astype(F32).T.astype(BF16).reshape(16, rows, 128)

    z_step(0)
    y_step(1)
    z_step(1)
    y_step(2)
    z_step(2)
    y_step(3)
    z_step(3)
    y_step(4)
    z_step(4)
    for copy in c_copies:
        copy.arrived()
    xn[:, :, 0:128] = turned(acts[0].reshape(128, d))
    y_step(5)
    xn[:, :, 128:256] = turned(acts[1].reshape(128, d))
    y_step(6)
    xc[:, :, 0:128] = turned(acts[2].reshape(128, d))
    for way in DIRS:
        last = {sub: max(f for q, f in Y_ITEMS[way] if q == sub) for sub in (0, 1)}
        for sub in (0, 1):
            y_copies[way, sub, last[sub]].arrived()

    lane = lax.broadcasted_iota(jnp.int32, (128, 128), 1)

    def iterate(m, cot):
        normed = acts[m].reshape(128, d)

        def part(lo, hi):
            return w[:, :, :, lo:hi].reshape(d, hi - lo)

        def gate(hidden, back):
            sigma = jax.nn.sigmoid(hidden)
            return hidden * sigma, back * sigma * (1.0 + hidden * (1.0 - sigma))

        hidden_out, back_in = gate(dot(normed, part(0, 256)), dot(cot, part(256, 512)))
        rest = part(512, 640)
        rest_out, rest_in = gate(dot(normed, rest), pltpu.roll(dot(cot, rest), 96, 1))
        rest_out = jnp.where(lane < 32, rest_out, 0.0)
        rest_in = jnp.where(lane < 32, rest_in, 0.0)
        at_m = slice(128 * m, 128 * (m + 1))
        back_in = back_in.astype(BF16)
        rest_in = rest_in.astype(BF16)
        bm[at_m, :] = back_in
        br[at_m, :] = rest_in
        hm[at_m, :] = hidden_out.astype(BF16)
        hr[at_m, :] = pltpu.roll(rest_out, 32, 1).astype(BF16)
        term = []
        step = 896
        wide = part(0, 256)
        for k in range(0, d, step):
            partial = dot_t(back_in, wide[k : k + step]) + dot_t(rest_in, rest[k : k + step])
            pb[m, :, :, :, k : k + step] = partial.astype(BF16).reshape(8, 2, 8, step)
            term.append(
                jnp.sum(partial * normed[:, k : k + step].astype(F32), axis=0, keepdims=True)
            )
        return jnp.concatenate(term, axis=1)

    def sum_cores(m):
        return Copy(pb.at[m, :, 1 - c], rc.at[m], rc.at[m], pair_c)

    def sum_out(m, first):
        first.arrived()
        qb[m] = (pb[m, :, c].astype(F32) + rc[m].astype(F32)).astype(BF16)
        return [
            Copy(qb.at[m, mod(z + k, 8)], rz.at[m, k], rz.at[m, k], at_z(k)) for k in range(1, 8)
        ]

    def sum_in(m, parts):
        for copy in parts:
            copy.arrived()
        total = qb[m, z].astype(F32)
        for k in range(1, 8):
            total = total + rz[m, k].astype(F32)
        st[m] = total.astype(BF16)
        return Copy(st.at[m], sr.at[m], sr.at[m], pair_l)

    def sum_end(m, last, cot):
        last.arrived()
        gained = (st[m].astype(F32) + sr[m].astype(F32)) * gain_wide
        scaled, reciprocal = own_state(m)
        back_state = reciprocal * (
            gained - scaled * jnp.mean(gained * scaled, axis=-1, keepdims=True)
        )
        return (cot.astype(F32) + back_state).astype(BF16)

    gain_term = iterate(0, acts[2].reshape(128, d))
    last = sum_in(0, sum_out(0, sum_cores(0)))
    res[...] = sum_end(0, last, acts[2, z, c])
    hand = Copy(res, cots.at[z, c], cots.at[z, c], before)
    hand.arrived()

    def cots_to_core(row):
        return Copy(cots.at[row, c], cots.at[row, c], cots.at[row, 1 - c], pair_c)

    spread = [
        Copy(cots.at[z, c], cots.at[z, c], cots.at[mod(z - k, 8), c], at_z(k))
        for k in (4, 3, 5, 2, 6, 1, 7)
    ]
    across = [cots_to_core(z)]
    for k, copy in zip((4, 3, 5, 2, 6, 1, 7), spread):
        copy.arrived()
        across.append(cots_to_core(mod(z - k, 8)))
    for copy in across:
        copy.arrived()

    gain_term = gain_term + iterate(1, cots[...].reshape(128, d))
    first = sum_cores(1)
    ga[0] = gain_term * scale / gain_wide
    gain_c = Copy(ga.at[0], ga.at[1], ga.at[1], pair_c)
    xc[:, :, 128:256] = turned(cots[...].reshape(128, d))

    def terms(row, at_h):
        k = row * 2 + at_h
        left_n, left_c = xn[k], xc[k]
        return (
            dot(left_n, bm[...]) * scale,
            dot(left_c, hm[...]) * scale,
            (dot(left_n, br[...]) + dot(left_c, hr[...])) * scale,
        )

    LANES = ((0, 256), (256, 512), (512, 640))
    g_copies = {}

    def g_step(i):
        for way in DIRS:
            sub, far = G_ITEMS[way][i]
            value = terms(mod(y + way * far, 8), g if sub else h)
            n = 0 if way == 1 else 1
            if (way, sub, far + 1) in g_copies:
                k = G_ITEMS[way].index((sub, far + 1))
                g_copies[way, sub, far + 1].arrived()
                value = [t + gr[n, k, :, a:b].astype(F32) for t, (a, b) in zip(value, LANES)]
            for t, (a, b) in zip(value, LANES):
                gs[n, i, :, a:b] = t.astype(BF16)
            g_copies[way, sub, far] = Copy(gs.at[n, i], gr.at[n, i], gr.at[n, i], at_y(way))

    def g_end(sub):
        value = terms(y, g if sub else h)
        for n, way in enumerate(DIRS):
            g_copies[way, sub, 1].arrived()
            k = G_ITEMS[way].index((sub, 1))
            value = [t + gr[n, k, :, a:b].astype(F32) for t, (a, b) in zip(value, LANES)]
        return value

    g_step(0)
    parts = sum_out(1, first)
    g_step(1)
    gain_c.arrived()
    ga[2] = ga[0] + ga[1]
    gain_l = Copy(ga.at[2], ga.at[3], ga.at[3], pair_l)
    g_step(2)
    gain_l.arrived()
    ga[4] = ga[2] + ga[3]
    gain_h = Copy(ga.at[4], ga.at[5], ga.at[5], pair_h)
    last = sum_in(1, parts)
    g_step(3)
    gain_h.arrived()
    gz[z] = ga[4] + ga[5]
    gain_z = [Copy(gz.at[z], gz.at[z], gz.at[mod(z - k, 8)], at_z(k)) for k in range(1, 8)]
    result = sum_end(1, last, cots[z, c])
    cot_out[0] = jnp.where(l == 0, result[0:4].astype(F32), result[4:8].astype(F32)).astype(BF16)
    g_step(4)
    for copy in gain_z:
        copy.arrived()
    gy[y] = jnp.sum(gz[...], axis=0)
    gain_y = [Copy(gy.at[y], gy.at[y], gy.at[mod(y - k, 8)], at_y(k)) for k in range(1, 8)]
    g_step(5)
    for copy in gain_y:
        copy.arrived()
    gain_out[...] = jnp.sum(gy[...], axis=0)
    g_step(6)

    for t, (a, b) in zip(g_end(1), LANES):
        fs[:, a:b] = t.astype(BF16)
    final = Copy(fs, fr, fr, pair_h)
    up_main, down_main, rest = g_end(0)
    final.arrived()
    up_out[:, 0:256] = (up_main + fr[:, 0:256].astype(F32)).astype(BF16)
    rest = rest + fr[:, 512:640].astype(F32)
    up_out[:, 256:288] = rest[:, 0:32].astype(BF16)
    down_out[0:256, :] = (down_main + fr[:, 256:512].astype(F32)).T.astype(BF16)
    down_out[256:288, :] = rest.T[32:64, :].astype(BF16)

    assert count[0] == N_COPIES, count[0]
    for copy in pending:
        copy.out.wait_send()


N_COPIES = 98


def on_device(scale, saved_states, cotangent_in, lengths, gain, up_weight, down_weight):
    d = gain.shape[0]
    rows, cols = up_weight.shape
    vmem = pl.BlockSpec(memory_space=pltpu.VMEM)
    outs = pl.pallas_call(
        functools.partial(kernel, scale),
        out_shape=(
            jax.ShapeDtypeStruct((1, 4, d), BF16),
            jax.ShapeDtypeStruct((rows, cols), BF16),
            jax.ShapeDtypeStruct((cols, rows), BF16),
            jax.ShapeDtypeStruct((1, d), F32),
        ),
        in_specs=[vmem, vmem, pl.BlockSpec(memory_space=pltpu.SMEM), vmem, vmem, vmem],
        out_specs=(vmem,) * 4,
        scratch_shapes=[
            pltpu.VMEM((8, 2, rows, 640), BF16),
            pltpu.VMEM((2, 2, 4, d), BF16),
            pltpu.VMEM((2, 4, d), BF16),
            pltpu.VMEM((3, 8, 2, 8, d), BF16),
            pltpu.VMEM((8, 2, 8, d), BF16),
            pltpu.VMEM((16, rows, 256), BF16),
            pltpu.VMEM((16, rows, 256), BF16),
            pltpu.VMEM((256, 256), BF16),
            pltpu.VMEM((256, 256), BF16),
            pltpu.VMEM((256, 128), BF16),
            pltpu.VMEM((256, 128), BF16),
            pltpu.VMEM((2, 8, 2, 8, d), BF16),
            pltpu.VMEM((2, 8, 8, d), BF16),
            pltpu.VMEM((2, 8, 8, d), BF16),
            pltpu.VMEM((2, 8, 8, d), BF16),
            pltpu.VMEM((2, 8, d), BF16),
            pltpu.VMEM((2, 8, d), BF16),
            pltpu.VMEM((8, d), BF16),
            pltpu.VMEM((2, 7, rows, 640), BF16),
            pltpu.VMEM((2, 7, rows, 640), BF16),
            pltpu.VMEM((rows, 640), BF16),
            pltpu.VMEM((rows, 640), BF16),
            pltpu.VMEM((6, 1, d), F32),
            pltpu.VMEM((8, 1, d), F32),
            pltpu.VMEM((8, 1, d), F32),
            pltpu.SemaphoreType.DMA((N_COPIES,)),
            pltpu.SemaphoreType.DMA((N_COPIES,)),
        ],
        compiler_params=pltpu.CompilerParams(
            collective_id=0, has_side_effects=True, vmem_limit_bytes=56 * 2**20
        ),
    )(saved_states, cotangent_in, lengths, gain[None], up_weight, down_weight)
    return outs[0], outs[1], outs[2], outs[3][0]


def solution(mesh):
    placed = (
        P("section", None, "dp", None),
        P("section", "dp", None),
        P("section"),
        P(),
        P("section", "dp"),
        P("dp", "section"),
    )
    scale = 1.0 / math.sqrt(2 * 128 * mesh.shape["section"])
    return jax.shard_map(
        functools.partial(on_device, scale),
        mesh=mesh,
        in_specs=placed,
        out_specs=(P("section", "dp", None), P("section", "dp"), P("dp", "section"), P()),
        check_vma=False,
    )
```

time: 1160 us -> 140 us (0.12)
  waiting for transfers between devices: 985 us -> 0 us
  Pallas kernels: 0 us -> 129 us
  blocking collectives: 116 us -> 0 us
  matrix products: 17 us -> 0 us
  between operations: 15 us -> 1.29 us
    psum x2 -> x0, waiting for transfers between devices: 445 us -> none  [back_iteration(): lax.psum(partial_value.astype(jnp.bfloat16), 'dp').astype(jnp.float32)]
    unnamed x9 -> x0, waiting for transfers between devices: 326 us -> none
    all_gather x3 -> x0, waiting for transfers between devices: 201 us -> none  [the longest x1 88.4 us: on_device(): lax.all_gather(down_weight, 'section', axis=1, tiled=True)]
    pallas_call x0 -> x1, Pallas kernels: none -> 129 us  [on_device(): pl.pallas_call(functools.partial(kernel, scale), out_shape=(jax.ShapeDtyp...]
    psum x1 -> x0, blocking collectives: 71.8 us -> none  [on_device(): gain_sum = lax.psum(gain_total * scale, 'section')]
    all_gather x1 -> x0, blocking collectives: 44.2 us -> none  [on_device(): lax.all_gather(cotangent_in, 'dp', axis=1, tiled=True)]
    dot_general x10 -> x0, matrix products: 17 us -> none  [the longest x4 6.76 us: contract_rows(): lax.dot_general(left, right, (((0,), (0,)), ((), ())), preferred_element_...]
    ppermute x1 -> x0, waiting for transfers between devices: 13.4 us -> none  [passed_along(): return lax.ppermute(block, axis, route)]
  transfers between devices with their start and end apart: 8 -> 0, of which waited for: 8 -> 0; matrix products, arithmetic and copies ran while one was open for 2% -> 0% of each run, Pallas kernels for 0% -> 0%
where the time goes in v1:
time: 140 us; the launch traced here: 138 us
  Pallas kernels  129 us (92%)
  local copies, waits for them, and re-layouts  5.94 us (4%)
    pallas_call x1, Pallas kernels, on_device(): pl.pallas_call(functools.partial(kernel, scale), out_shape=(jax.ShapeDtyp...  129 us
    unnamed x8, local copies, waits for them, and re-layouts  4.64 us

profile of v1, /device:TPU:6, one launch (start us, length us, event | category | flops | bytes accessed | tf_op | source)
XLA Modules:
  0.0 137.7 jit_solution(597130320373686911)
XLA Ops:
  1.3 1.3 broadcast_in_dim.3.gain
  2.6 1.7 %copy.10.down = bf16[288,168]{1,0:T(8,128)(2,1)} copy(bf16[288,168]{0,1:T(8,128)(2,1)} %param.11) | data formatting | bytes 193536 | tf_op args[5]
  4.2 129.1 %shard_map.93 = (bf16[1,4,2688]{2,1,0:T(4,128)(2,1)}, bf16[168,288]{1,0:T(8,128)(2,1)}, bf16[288,168]{1,0:T(8,128)(2,1)}, f32[1,2688]{1,0:T(1,128)}) custom-call(bf16[1,2,4,2688]{3,2,1,0:T(4,128)(2,1)} %states.1, bf16[1,4,2688]{2,1,0:T(4,128)(2,1)} %cot_in.1, s32[1]{0:T(128)S(6)} %copy.14.lengths, bf16[1,2688]{1,0:T(2,128)(2,1)} %broadcast_in_dim.3.gain, ...), custom_call_target="tpu_custom_call" | custom-call | tf_op jit(solution)/shard_map/pallas_call | solution.py:365
  133.4 1.3 reduce
  134.7 0.0 copy-start.1
  134.7 0.0 copy-start
  134.7 1.7 %copy.11 = bf16[288,168]{0,1:T(8,128)(2,1)} copy(bf16[288,168]{1,0:T(8,128)(2,1)} %get-tuple-element.14) | data formatting | bytes 193536
  136.4 0.0 copy-done.1
  136.4 0.6 copy.15
  137.0 0.0 copy-done
  137.0 0.7 copy.16
Async XLA Ops:
  134.7 1.7 %copy-start.1 = (bf16[1,4,2688]{2,1,0:T(4,128)(2,1)S(1)}, bf16[1,4,2688]{2,1,0:T(4,128)(2,1)}, u32[]{:S(2)}) copy-start(bf16[1,4,2688]{2,1,0:T(4,128)(2,1)} %get-tuple-element.20) | copy-start | bytes 64516
  134.7 2.3 %copy-start = (bf16[168,288]{1,0:T(8,128)(2,1)S(1)}, bf16[168,288]{1,0:T(8,128)(2,1)}, u32[]{:S(2)}) copy-start(bf16[168,288]{1,0:T(8,128)(2,1)} %get-tuple-element.21) | copy-start | bytes 290308

commit v2 on v1

v2 whole, which is shorter than its diff:
```python
import functools
import math

import jax
import jax.numpy as jnp
from jax import lax
from jax.experimental import pallas as pl
from jax.experimental.pallas import tpu as pltpu
from jax.sharding import PartitionSpec as P

MESH = pl.DeviceIdType.MESH
F32, BF16 = jnp.float32, jnp.bfloat16
epsilon = 1e-06

A_ITEMS = {
    1: ((0, 0), (1, 0), (0, 1), (1, 1), (0, 2), (1, 2), (0, 3)),
    -1: ((0, 0), (1, 0), (0, 1), (1, 1), (0, 2), (1, 2), (1, 3)),
}
GA_ITEMS = {
    1: ((0, 4), (1, 3), (0, 3), (1, 2), (0, 2), (1, 1), (0, 1)),
    -1: ((1, 4), (0, 3), (1, 3), (0, 2), (1, 2), (0, 1), (1, 1)),
}
REACH = {1: 4, -1: 3}
DIRS = (1, -1)
N_COPIES = 160


def mod(a, n):
    return lax.rem(a + n, n)


def dot(a, b):
    return jnp.dot(a, b, preferred_element_type=F32)


def dot_t(a, b):
    return lax.dot_general(a, b, (((1,), (1,)), ((), ())), preferred_element_type=F32)


def b_pieces(way, far, last):
    return (0, 1) if far != last else (0,) if way == 1 else (1,)


def folded(rest):
    return jnp.concatenate([rest[0:80] + pltpu.roll(rest[88:168], 64, 1), rest[80:88]], axis=0)


def kernel(
    scale, states, cot_in, lengths, gain, up, down,
    cot_out, up_out, down_out, gain_out,
    wa, wb0, wb1, wr, e_s, e_c, n_s, n_c, nb, acts, cots, xn, xc, bm, hm, br, hr,
    pb, rc, qb, zs, rz, st, sr,
    gas, gar, gx0, gx1, hx0, hx1, gs0, gs1, gr0, gr1, fs, fr,
    ga, gz, gy, send, recv,
):
    s, p = lax.axis_index("section"), lax.axis_index("dp")
    y, h = lax.div(s, 2), lax.rem(s, 2)
    z, l, c = lax.div(p, 4), lax.rem(lax.div(p, 2), 2), lax.rem(p, 2)
    g = 1 - h
    wb, gx, hx, gs, gr = (wb0, wb1), (gx0, gx1), (hx0, hx1), (gs0, gs1), (gr0, gr1)

    def at(section=None, dp=None):
        return {"section": s if section is None else section, "dp": p if dp is None else dp}

    def at_y(k):
        return at(section=mod(y + k, 8) * 2 + h)

    def at_z(k):
        return at(dp=mod(z + k, 8) * 4 + l * 2 + c)

    other_l = p + 2 - 4 * l
    pair_h = at(section=s + 1 - 2 * h)
    pair_l = at(dp=other_l)
    pair_c = at(dp=p + 1 - 2 * c)
    before = at(section=mod(s - 1, 16))
    before_l = at(section=mod(s - 1, 16), dp=other_l)
    cross = mod(s - 1 + 2 * h, 16)

    pending = []

    class Copy:
        def __init__(self, src, dst, landing, device):
            k = len(pending)
            self.out = pltpu.make_async_remote_copy(
                src_ref=src, dst_ref=dst, send_sem=send.at[k], recv_sem=recv.at[k],
                device_id=device, device_id_type=MESH,
            )
            self.arrival = pltpu.make_async_remote_copy(
                src_ref=src, dst_ref=landing, send_sem=send.at[k], recv_sem=recv.at[k],
                device_id=device, device_id_type=MESH,
            )
            pending.append(self)
            self.out.start()

        def arrived(self):
            self.arrival.wait_recv()

    barrier = pltpu.get_barrier_semaphore()
    partners = [at_y(k) for k in range(1, 8)] + [at_z(k) for k in range(1, 8)]
    partners += [pair_h, pair_l, pair_c, at(section=cross)]
    partners += [at(section=s + 1 - 2 * h, dp=other_l), at(section=cross, dp=other_l)]
    for device in partners:
        pl.semaphore_signal(barrier, inc=1, device_id=device, device_id_type=MESH)

    rows = up.shape[0]
    wa[y, h] = up[:, 0:256]
    wb0[y, h, 0:rows, :] = down[:, 0:128]
    wb1[y, h] = down[:, 128:256]
    wb0[y, h, rows : rows + 88, :] = folded(
        jnp.concatenate(
            [up[:, 256:288].astype(F32), down[:, 256:288].astype(F32), jnp.zeros((rows, 64), F32)],
            axis=1,
        )
    ).astype(BF16)
    e_s[l] = states[0]
    e_c[l] = cot_in[0]

    pl.semaphore_wait(barrier, len(partners))

    swap_w = Copy(wa.at[y, h], wa.at[y, h], wa.at[y, g], pair_h)
    a_copies, b_copies, x_copies = {}, {}, []

    def a_step(i):
        for way in DIRS:
            sub, far = A_ITEMS[way][i]
            if far > 0:
                a_copies[way, sub, far - 1].arrived()
            elif sub == 1 and way == 1:
                swap_w.arrived()
            row = mod(y - way * far, 8)
            land = mod(y - way * (far + 1), 8)
            at_h = g if sub else h
            a_copies[way, sub, far] = Copy(wa.at[row, at_h], wa.at[row, at_h], wa.at[land, at_h], at_y(way))

    def b_across(row, j):
        x_copies.append(Copy(wb[j].at[row, h], wb[j].at[row, h], wb[j].at[row, g], pair_h))

    def b_step(far):
        for way in DIRS:
            row = mod(y - way * far, 8)
            land = mod(y - way * (far + 1), 8)
            for j in (0, 1):
                came = far > 0 and j in b_pieces(way, far - 1, 3)
                if came:
                    b_copies[way, j, far - 1].arrived()
                if far < 4 and j in b_pieces(way, far, 3):
                    b_copies[way, j, far] = Copy(
                        wb[j].at[row, h], wb[j].at[row, h], wb[j].at[land, h], at_y(way)
                    )
                if came:
                    b_across(row, j)

    b_step(0)
    a_step(0)
    swap_s = Copy(e_s.at[l], e_s.at[l], e_s.at[1 - l], pair_l)
    swap_c = Copy(e_c.at[l], e_c.at[l], e_c.at[1 - l], pair_l)
    a_step(1)
    b_across(y, 0)
    b_across(y, 1)

    d = gain.shape[0]
    gain_wide = gain[...].astype(F32).reshape(1, d)
    swap_s.arrived()
    swap_c.arrived()
    in_chunk = lax.broadcasted_iota(jnp.int32, (8, 1), 0)
    position = z * 16 + c * 4 + jnp.where(in_chunk >= 4, in_chunk + 4, in_chunk)

    def scaled_of(first, second):
        values = jnp.concatenate([first.astype(F32), second.astype(F32)], axis=0)
        reciprocal = lax.rsqrt(jnp.mean(values * values, axis=-1, keepdims=True) + epsilon)
        return values * reciprocal, reciprocal

    for m in range(2):
        acts[m, z, c] = (scaled_of(e_s[0, m], e_s[1, m])[0] * gain_wide).astype(BF16)
    raw = jnp.concatenate([e_c[0].astype(F32), e_c[1].astype(F32)], axis=0)
    acts[2, z, c] = jnp.where(position < lengths[0], raw, 0.0).astype(BF16)

    z_copies, c_copies = {}, []

    def ring_z(step, block, copies, to_core):
        for way in DIRS:
            if step > REACH[way]:
                continue
            row = mod(z - way * step, 8)
            if step > 0:
                copies[way, step - 1].arrived()
            if step < REACH[way]:
                land = mod(z - way * (step + 1), 8)
                copies[way, step] = Copy(block(row, c), block(row, c), block(land, c), at_z(way))
            if step > 0 or way == 1:
                to_core.append(Copy(block(row, c), block(row, c), block(row, 1 - c), pair_c))

    def z_step(step):
        ring_z(step, lambda row, core: acts.at[:, row, core], z_copies, c_copies)

    def turned(value):
        return value.astype(F32).T.astype(BF16).reshape(16, rows, 128)

    z_step(0)
    next_s = Copy(e_s.at[:, 0], n_s, n_s, before)
    next_c = Copy(acts.at[2, z, c], n_c, n_c, before)
    b_step(1)
    z_step(1)
    a_step(2)
    b_step(2)
    z_step(2)
    a_step(3)
    z_step(3)
    b_step(3)
    z_step(4)
    a_step(4)
    for copy in c_copies:
        copy.arrived()
    xn[:, :, 0:128] = turned(acts[0].reshape(128, d))
    b_step(4)
    a_step(5)
    xn[:, :, 128:256] = turned(acts[1].reshape(128, d))
    a_step(6)
    xc[:, :, 0:128] = turned(acts[2].reshape(128, d))
    next_s.arrived()
    next_c.arrived()
    for copy in x_copies:
        copy.arrived()
    for way in DIRS:
        for sub in (0, 1):
            last = max(f for q, f in A_ITEMS[way] if q == sub)
            a_copies[way, sub, last].arrived()
    for row in range(8):
        for k in range(2):
            fold = wb0[row, k, rows : rows + 88, :].astype(F32)
            wr[row, k] = jnp.concatenate([fold, pltpu.roll(fold[0:80], 64, 1)], axis=0).astype(BF16)

    lane = lax.broadcasted_iota(jnp.int32, (128, 128), 1)

    def gate(hidden, back):
        sigma = jax.nn.sigmoid(hidden)
        return hidden * sigma, back * sigma * (1.0 + hidden * (1.0 - sigma))

    def hidden_side(m, cot):
        normed = acts[m].reshape(128, d)
        down_main = jnp.concatenate(
            [wb0[:, :, 0:rows, :].reshape(d, 128), wb1[...].reshape(d, 128)], axis=1
        )
        hidden_out, back_in = gate(dot(normed, wa[...].reshape(d, 256)), dot(cot, down_main))
        rest = wr[...].reshape(d, 128)
        rest_out, rest_in = gate(dot(normed, rest), pltpu.roll(dot(cot, rest), 96, 1))
        rest_out = jnp.where(lane < 32, rest_out, 0.0)
        rest_in = jnp.where(lane < 32, rest_in, 0.0)
        at_m = slice(128 * m, 128 * (m + 1))
        bm[at_m, :] = back_in.astype(BF16)
        br[at_m, :] = rest_in.astype(BF16)
        hm[at_m, :] = hidden_out.astype(BF16)
        hr[at_m, :] = pltpu.roll(rest_out, 32, 1).astype(BF16)

    def back_side(m):
        normed = acts[m].reshape(128, d)
        at_m = slice(128 * m, 128 * (m + 1))
        back_in, rest_in = bm[at_m, :], br[at_m, :]
        wide, rest = wa[...].reshape(d, 256), wr[...].reshape(d, 128)
        term = []
        step = 896
        for k in range(0, d, step):
            partial = dot_t(back_in, wide[k : k + step]) + dot_t(rest_in, rest[k : k + step])
            pb[m, :, :, :, k : k + step] = partial.astype(BF16).reshape(8, 2, 8, step)
            term.append(
                jnp.sum(partial * normed[:, k : k + step].astype(F32), axis=0, keepdims=True)
            )
        return jnp.concatenate(term, axis=1), Copy(pb.at[m, :, 1 - c], rc.at[m], rc.at[m], pair_c)

    s_copies = {}

    def sum_step(m, step, first):
        if step == 0:
            first.arrived()
            qb[m] = (pb[m, :, c].astype(F32) + rc[m].astype(F32)).astype(BF16)
        for n, way in enumerate(DIRS):
            far = REACH[way] - step
            if far < 1:
                continue
            source = qb.at[m, mod(z + way * far, 8)]
            if step > 0:
                s_copies[m, way, step - 1].arrived()
                total = source[...].astype(F32) + rz[m, n, step - 1].astype(F32)
                source = zs.at[m, n, step]
                source[...] = total.astype(BF16)
            s_copies[m, way, step] = Copy(source, rz.at[m, n, step], rz.at[m, n, step], at_z(way))

    def sum_in(m):
        s_copies[m, 1, 3].arrived()
        s_copies[m, -1, 2].arrived()
        total = qb[m, z].astype(F32) + rz[m, 0, 3].astype(F32) + rz[m, 1, 2].astype(F32)
        st[m] = total.astype(BF16)

    def norm_side(back_normed, scaled, reciprocal, cot):
        gained = back_normed * gain_wide
        back_state = reciprocal * (
            gained - scaled * jnp.mean(gained * scaled, axis=-1, keepdims=True)
        )
        return (cot.astype(F32) + back_state).astype(BF16)

    hidden_side(0, acts[2].reshape(128, d))
    gain_term, first = back_side(0)
    for step in range(4):
        sum_step(0, step, first)
    scaled, reciprocal = scaled_of(n_s[0], n_s[1])
    sum_in(0)
    hands = [
        Copy(st.at[0], nb.at[l], nb.at[l], before),
        Copy(st.at[0], nb.at[l], nb.at[1 - l], before_l),
    ]
    for copy in hands:
        copy.arrived()
    cots[z, c] = norm_side(nb[0].astype(F32) + nb[1].astype(F32), scaled, reciprocal, n_c[...])
    r_copies, across = {}, []
    for step in range(5):
        ring_z(step, lambda row, core: cots.at[row, core], r_copies, across)
    for copy in across:
        copy.arrived()

    hidden_side(1, cots[...].reshape(128, d))
    ga_copies, gx_copies, gb_copies = {}, {}, {}

    def ga_step(i):
        for n, way in enumerate(DIRS):
            sub, far = GA_ITEMS[way][i]
            value = dot(xn[mod(y + way * far, 8) * 2 + (g if sub else h)], bm[...]) * scale
            if (way, sub, far + 1) in ga_copies:
                k = GA_ITEMS[way].index((sub, far + 1))
                ga_copies[way, sub, far + 1].arrived()
                value = value + gar[n, k].astype(F32)
            gas[n, i] = value.astype(BF16)
            ga_copies[way, sub, far] = Copy(gas.at[n, i], gar.at[n, i], gar.at[n, i], at_y(way))

    def ga_end(sub):
        value = dot(xn[y * 2 + (g if sub else h)], bm[...]) * scale
        for n, way in enumerate(DIRS):
            ga_copies[way, sub, 1].arrived()
            value = value + gar[n, GA_ITEMS[way].index((sub, 1))].astype(F32)
        return value

    def b_terms(far, at_h):
        k = mod(y + far, 8) * 2 + at_h
        left_n, left_c = xn[k], xc[k]
        main = dot(left_c, hm[...]) * scale
        rest = (dot(left_n, br[...]) + dot(left_c, hr[...])) * scale
        return [jnp.concatenate([main[:, 0:128], folded(rest)], axis=0), main[:, 128:256]]

    def gx_step(far):
        k = far + 3
        for j, value in enumerate(b_terms(far, g)):
            gx[j][k] = value.astype(BF16)
            gx_copies[far, j] = Copy(gx[j].at[k], hx[j].at[k], hx[j].at[k], pair_h)

    def b_pair(far):
        value = b_terms(far, h)
        for j in (0, 1):
            gx_copies[far, j].arrived()
            value[j] = value[j] + hx[j][far + 3].astype(F32)
        return value

    def gb_step(far):
        if far == 4:
            pair = b_pair(4)
        for n, way in enumerate(DIRS):
            if far < 4:
                pair = b_pair(way * far)
            for j in b_pieces(way, far, 4):
                value = pair[j]
                if (way, j, far + 1) in gb_copies:
                    gb_copies[way, j, far + 1].arrived()
                    value = value + gr[j][n, far + 1].astype(F32)
                gs[j][n, far] = value.astype(BF16)
                gb_copies[way, j, far] = Copy(
                    gs[j].at[n, far], gr[j].at[n, far], gr[j].at[n, far], at_y(way)
                )

    ga_step(0)
    ga_step(1)
    xc[:, :, 128:256] = turned(cots[...].reshape(128, d))
    gx_step(4)
    gx_step(3)
    gx_step(-3)
    term, first = back_side(1)
    ga[0] = (gain_term + term) * scale / gain_wide
    gain_c = Copy(ga.at[0], ga.at[1], ga.at[1], pair_c)
    ga_step(2)
    gx_step(2)
    gx_step(-2)
    gb_step(4)
    sum_step(1, 0, first)
    gx_step(1)
    gx_step(-1)
    gx_step(0)
    ga_step(3)
    sum_step(1, 1, first)
    gain_c.arrived()
    ga[2] = ga[0] + ga[1]
    gain_l = Copy(ga.at[2], ga.at[3], ga.at[3], pair_l)
    gb_step(3)
    sum_step(1, 2, first)
    gain_l.arrived()
    ga[4] = ga[2] + ga[3]
    gain_h = Copy(ga.at[4], ga.at[5], ga.at[5], pair_h)
    ga_step(4)
    sum_step(1, 3, first)
    gain_h.arrived()
    gz[z] = ga[4] + ga[5]
    gain_z = [Copy(gz.at[z], gz.at[z], gz.at[mod(z - k, 8)], at_z(k)) for k in range(1, 8)]
    gb_step(2)
    sum_in(1)
    last = Copy(st.at[1], sr, sr, pair_l)
    ga_step(5)
    for copy in gain_z:
        copy.arrived()
    gy[y] = jnp.sum(gz[...], axis=0)
    gain_y = [Copy(gy.at[y], gy.at[y], gy.at[mod(y - k, 8)], at_y(k)) for k in range(1, 8)]
    ga_step(6)
    gb_step(1)
    scaled, reciprocal = scaled_of(e_s[0, 1], e_s[1, 1])
    last.arrived()
    result = norm_side(st[1].astype(F32) + sr[...].astype(F32), scaled, reciprocal, cots[z, c])
    cot_out[0] = jnp.where(l == 0, result[0:4].astype(F32), result[4:8].astype(F32)).astype(BF16)
    for copy in gain_y:
        copy.arrived()
    gain_out[...] = jnp.sum(gy[...], axis=0).reshape(d)

    fs[...] = ga_end(1).astype(BF16)
    final = Copy(fs, fr, fr, pair_h)
    up_main = ga_end(0)
    down_main, fold = None, None
    pair = b_pair(0)
    for j in (0, 1):
        for n, way in enumerate(DIRS):
            gb_copies[way, j, 1].arrived()
            pair[j] = pair[j] + gr[j][n, 1].astype(F32)
    down_out[:, 0:128] = pair[0][0:rows].astype(BF16)
    down_out[:, 128:256] = pair[1].astype(BF16)
    fold = pair[0][rows : rows + 88]
    rest = jnp.concatenate([fold, pltpu.roll(fold[0:80], 64, 1)], axis=0)
    up_out[:, 256:288] = rest[:, 0:32].astype(BF16)
    down_out[:, 256:288] = rest[:, 32:64].astype(BF16)
    final.arrived()
    up_out[:, 0:256] = (up_main + fr[...].astype(F32)).astype(BF16)

    assert len(pending) == N_COPIES, len(pending)
    for copy in pending:
        copy.out.wait_send()


def on_device(scale, saved_states, cotangent_in, lengths, gain, up_weight, down_weight):
    d = gain.shape[0]
    rows, cols = up_weight.shape
    vmem = pl.BlockSpec(memory_space=pltpu.VMEM)
    scratch = dict(
        wa=(8, 2, rows, 256), wb0=(8, 2, rows + 88, 128), wb1=(8, 2, rows, 128), wr=(8, 2, rows, 128),
        e_s=(2, 2, 4, d), e_c=(2, 4, d), n_s=(2, 4, d), n_c=(8, d), nb=(2, 8, d),
        acts=(3, 8, 2, 8, d), cots=(8, 2, 8, d), xn=(16, rows, 256), xc=(16, rows, 256),
        bm=(256, 256), hm=(256, 256), br=(256, 128), hr=(256, 128),
        pb=(2, 8, 2, 8, d), rc=(2, 8, 8, d), qb=(2, 8, 8, d), zs=(2, 2, 4, 8, d), rz=(2, 2, 4, 8, d),
        st=(2, 8, d), sr=(8, d),
        gas=(2, 7, rows, 256), gar=(2, 7, rows, 256),
        gx0=(8, rows + 88, 128), gx1=(8, rows, 128), hx0=(8, rows + 88, 128), hx1=(8, rows, 128),
        gs0=(2, 5, rows + 88, 128), gs1=(2, 5, rows, 128),
        gr0=(2, 5, rows + 88, 128), gr1=(2, 5, rows, 128),
        fs=(rows, 256), fr=(rows, 256),
    )
    outs = pl.pallas_call(
        functools.partial(kernel, scale),
        out_shape=(
            jax.ShapeDtypeStruct((1, 4, d), BF16),
            jax.ShapeDtypeStruct((rows, cols), BF16),
            jax.ShapeDtypeStruct((rows, cols), BF16),
            jax.ShapeDtypeStruct((d,), F32),
        ),
        in_specs=[vmem, vmem, pl.BlockSpec(memory_space=pltpu.SMEM), vmem, vmem, vmem],
        out_specs=(vmem,) * 4,
        scratch_shapes=[pltpu.VMEM(shape, BF16) for shape in scratch.values()]
        + [pltpu.VMEM((n, 1, d), F32) for n in (6, 8, 8)]
        + [pltpu.SemaphoreType.DMA((N_COPIES,))] * 2,
        compiler_params=pltpu.CompilerParams(
            collective_id=0, has_side_effects=True, vmem_limit_bytes=56 * 2**20
        ),
    )(saved_states, cotangent_in, lengths, gain, up_weight, down_weight.T)
    return outs[0], outs[1], outs[2].T, outs[3]


def solution(mesh):
    placed = (
        P("section", None, "dp", None),
        P("section", "dp", None),
        P("section"),
        P(),
        P("section", "dp"),
        P("dp", "section"),
    )
    scale = 1.0 / math.sqrt(2 * 128 * mesh.shape["section"])
    return jax.shard_map(
        functools.partial(on_device, scale),
        mesh=mesh,
        in_specs=placed,
        out_specs=(P("section", "dp", None), P("section", "dp"), P("dp", "section"), P()),
        check_vma=False,
    )
```

time: 140 us -> 132 us (0.943)
  Pallas kernels: 129 us -> 125 us
  local copies, waits for them, and re-layouts: 5.94 us -> 4.26 us
    pallas_call x1, Pallas kernels: 129 us -> 125 us  [on_device(): pl.pallas_call(functools.partial(kernel, scale), out_shape=(jax.ShapeDtyp...]
where the time goes in v2:
time: 132 us; the launch traced here: 130 us
  Pallas kernels  125 us (95%)
  local copies, waits for them, and re-layouts  4.26 us (3%)
    pallas_call x1, Pallas kernels, on_device(): pl.pallas_call(functools.partial(kernel, scale), out_shape=(jax.ShapeDtyp...  125 us
    unnamed x8, local copies, waits for them, and re-layouts  4.26 us

profile of v2, /device:TPU:6, one launch (start us, length us, event | category | flops | bytes accessed | tf_op | source)
XLA Modules:
  0.0 130.4 jit_solution(7727563428029651038)
XLA Ops:
  1.3 124.8 %shard_map.93 = (bf16[1,4,2688]{2,1,0:T(4,128)(2,1)}, bf16[168,288]{1,0:T(8,128)(2,1)}, bf16[168,288]{1,0:T(8,128)(2,1)}, f32[2688]{0:T(1024)}) custom-call(bf16[1,2,4,2688]{3,2,1,0:T(4,128)(2,1)} %states.1, bf16[1,4,2688]{2,1,0:T(4,128)(2,1)} %cot_in.1, s32[1]{0:T(128)S(6)} %copy.14.lengths, bf16[2688]{0:T(1024)(128)(2,1)} %gain.1, bf16[168,288]{1,0:T(8,128)(2,1)} %up.1, ...), custom_call_target="tpu_custom_call" | custom-call | tf_op jit(solution)/shard_map/pallas_call | solution.py:467
  126.1 1.3 %copy.15 = bf16[1,4,2688]{2,1,0:T(4,128)(2,1)} copy(bf16[1,4,2688]{2,1,0:T(4,128)(2,1)} %get-tuple-element.16) | data formatting | bytes 43008
  127.5 0.0 copy-start
  127.5 1.6 %copy.16 = bf16[168,288]{1,0:T(8,128)(2,1)} copy(bf16[168,288]{1,0:T(8,128)(2,1)} %get-tuple-element.17) | data formatting | bytes 193536
  129.1 0.0 copy-done
  129.1 0.0 copy-start.1
  129.1 0.7 copy.17
  129.7 0.1 copy-done.1
  129.8 0.6 copy.18
Async XLA Ops:
  127.5 1.6 %copy-start = (bf16[168,288]{1,0:T(8,128)(2,1)S(1)}, bf16[168,288]{1,0:T(8,128)(2,1)}, u32[]{:S(2)}) copy-start(bf16[168,288]{1,0:T(8,128)(2,1)} %get-tuple-element.10) | copy-start | bytes 290308
  129.1 0.7 copy-start.1

commit v3 on v2

--- a/solution.py
+++ b/solution.py
@@ -20,9 +20,8 @@
     1: ((0, 4), (1, 3), (0, 3), (1, 2), (0, 2), (1, 1), (0, 1)),
     -1: ((1, 4), (0, 3), (1, 3), (0, 2), (1, 2), (0, 1), (1, 1)),
 }
-REACH = {1: 4, -1: 3}
 DIRS = (1, -1)
-N_COPIES = 160
+N_COPIES = 176
 
 
 def mod(a, n):
@@ -49,7 +48,7 @@
     scale, states, cot_in, lengths, gain, up, down,
     cot_out, up_out, down_out, gain_out,
     wa, wb0, wb1, wr, e_s, e_c, n_s, n_c, nb, acts, cots, xn, xc, bm, hm, br, hr,
-    pb, rc, qb, zs, rz, st, sr,
+    pb, rc, qb, rz, st, sr,
     gas, gar, gx0, gx1, hx0, hx1, gs0, gs1, gr0, gr1, fs, fr,
     ga, gz, gy, send, recv,
 ):
@@ -72,6 +71,7 @@
     pair_h = at(section=s + 1 - 2 * h)
     pair_l = at(dp=other_l)
     pair_c = at(dp=p + 1 - 2 * c)
+    pair_hl = at(section=s + 1 - 2 * h, dp=other_l)
     before = at(section=mod(s - 1, 16))
     before_l = at(section=mod(s - 1, 16), dp=other_l)
     cross = mod(s - 1 + 2 * h, 16)
@@ -98,7 +98,7 @@
     barrier = pltpu.get_barrier_semaphore()
     partners = [at_y(k) for k in range(1, 8)] + [at_z(k) for k in range(1, 8)]
     partners += [pair_h, pair_l, pair_c, at(section=cross)]
-    partners += [at(section=s + 1 - 2 * h, dp=other_l), at(section=cross, dp=other_l)]
+    partners += [pair_hl, at(section=cross, dp=other_l)]
     for device in partners:
         pl.semaphore_signal(barrier, inc=1, device_id=device, device_id_type=MESH)
 
@@ -117,6 +117,8 @@
 
     pl.semaphore_wait(barrier, len(partners))
 
+    swap_s = Copy(e_s.at[l], e_s.at[l], e_s.at[1 - l], pair_l)
+    swap_c = Copy(e_c.at[l], e_c.at[l], e_c.at[1 - l], pair_l)
     swap_w = Copy(wa.at[y, h], wa.at[y, h], wa.at[y, g], pair_h)
     a_copies, b_copies, x_copies = {}, {}, []
 
@@ -152,11 +154,9 @@
 
     b_step(0)
     a_step(0)
-    swap_s = Copy(e_s.at[l], e_s.at[l], e_s.at[1 - l], pair_l)
-    swap_c = Copy(e_c.at[l], e_c.at[l], e_c.at[1 - l], pair_l)
-    a_step(1)
     b_across(y, 0)
     b_across(y, 1)
+    b_step(1)
 
     d = gain.shape[0]
     gain_wide = gain[...].astype(F32).reshape(1, d)
@@ -171,60 +171,78 @@
         return values * reciprocal, reciprocal
 
     for m in range(2):
-        acts[m, z, c] = (scaled_of(e_s[0, m], e_s[1, m])[0] * gain_wide).astype(BF16)
+        acts[2 * m, z, c] = (scaled_of(e_s[0, m], e_s[1, m])[0] * gain_wide).astype(BF16)
     raw = jnp.concatenate([e_c[0].astype(F32), e_c[1].astype(F32)], axis=0)
-    acts[2, z, c] = jnp.where(position < lengths[0], raw, 0.0).astype(BF16)
-
+    acts[1, z, c] = jnp.where(position < lengths[0], raw, 0.0).astype(BF16)
+
+    FIRST, SECOND = slice(0, 2), slice(2, 3)
     z_copies, c_copies = {}, []
 
-    def ring_z(step, block, copies, to_core):
-        for way in DIRS:
-            if step > REACH[way]:
-                continue
-            row = mod(z - way * step, 8)
-            if step > 0:
-                copies[way, step - 1].arrived()
-            if step < REACH[way]:
-                land = mod(z - way * (step + 1), 8)
-                copies[way, step] = Copy(block(row, c), block(row, c), block(land, c), at_z(way))
-            if step > 0 or way == 1:
-                to_core.append(Copy(block(row, c), block(row, c), block(row, 1 - c), pair_c))
-
-    def z_step(step):
-        ring_z(step, lambda row, core: acts.at[:, row, core], z_copies, c_copies)
+    def act(part, row, core):
+        return acts.at[part, row, core]
+
+    def z_send(part, k, row, far):
+        row, land = mod(row, 8), mod(z - far, 8)
+        z_copies[part.start, far] = Copy(act(part, row, c), act(part, row, c), act(part, land, c), at_z(k))
+
+    def z_core(part, row):
+        row = mod(row, 8)
+        c_copies.append(Copy(act(part, row, c), act(part, row, c), act(part, row, 1 - c), pair_c))
+
+    def z_near(part):
+        for k in (2, -2, 1, -1):
+            z_send(part, k, z, k)
+        z_core(part, z)
+
+    def z_far(part):
+        z_copies[part.start, 2].arrived()
+        z_send(part, 2, z - 2, 4)
+        z_send(part, 1, z - 2, 3)
+        z_copies[part.start, -2].arrived()
+        z_send(part, -1, z + 2, -3)
+        for k in (2, -2, 1, -1):
+            if k in (1, -1):
+                z_copies[part.start, k].arrived()
+            z_core(part, z - k)
+
+    def z_last(part):
+        for k in (3, -3, 4):
+            z_copies[part.start, k].arrived()
+            z_core(part, z - k)
 
     def turned(value):
         return value.astype(F32).T.astype(BF16).reshape(16, rows, 128)
 
-    z_step(0)
+    z_near(FIRST)
+    z_near(SECOND)
+    a_step(2)
+    a_step(1)
     next_s = Copy(e_s.at[:, 0], n_s, n_s, before)
-    next_c = Copy(acts.at[2, z, c], n_c, n_c, before)
-    b_step(1)
-    z_step(1)
-    a_step(2)
+    next_c = Copy(acts.at[1, z, c], n_c, n_c, before)
     b_step(2)
-    z_step(2)
+    a_step(4)
+    z_far(FIRST)
     a_step(3)
-    z_step(3)
     b_step(3)
-    z_step(4)
-    a_step(4)
+    a_step(5)
+    z_far(SECOND)
+    b_step(4)
+    a_step(6)
+    z_last(FIRST)
+    z_last(SECOND)
     for copy in c_copies:
         copy.arrived()
     xn[:, :, 0:128] = turned(acts[0].reshape(128, d))
-    b_step(4)
-    a_step(5)
-    xn[:, :, 128:256] = turned(acts[1].reshape(128, d))
-    a_step(6)
-    xc[:, :, 0:128] = turned(acts[2].reshape(128, d))
+    xn[:, :, 128:256] = turned(acts[2].reshape(128, d))
+    xc[:, :, 0:128] = turned(acts[1].reshape(128, d))
     next_s.arrived()
     next_c.arrived()
-    for copy in x_copies:
-        copy.arrived()
     for way in DIRS:
         for sub in (0, 1):
             last = max(f for q, f in A_ITEMS[way] if q == sub)
             a_copies[way, sub, last].arrived()
+    for copy in x_copies:
+        copy.arrived()
     for row in range(8):
         for k in range(2):
             fold = wb0[row, k, rows : rows + 88, :].astype(F32)
@@ -237,7 +255,7 @@
         return hidden * sigma, back * sigma * (1.0 + hidden * (1.0 - sigma))
 
     def hidden_side(m, cot):
-        normed = acts[m].reshape(128, d)
+        normed = acts[2 * m].reshape(128, d)
         down_main = jnp.concatenate(
             [wb0[:, :, 0:rows, :].reshape(d, 128), wb1[...].reshape(d, 128)], axis=1
         )
@@ -253,7 +271,7 @@
         hr[at_m, :] = pltpu.roll(rest_out, 32, 1).astype(BF16)
 
     def back_side(m):
-        normed = acts[m].reshape(128, d)
+        normed = acts[2 * m].reshape(128, d)
         at_m = slice(128 * m, 128 * (m + 1))
         back_in, rest_in = bm[at_m, :], br[at_m, :]
         wide, rest = wa[...].reshape(d, 256), wr[...].reshape(d, 128)
@@ -267,28 +285,20 @@
             )
         return jnp.concatenate(term, axis=1), Copy(pb.at[m, :, 1 - c], rc.at[m], rc.at[m], pair_c)
 
-    s_copies = {}
-
-    def sum_step(m, step, first):
-        if step == 0:
-            first.arrived()
-            qb[m] = (pb[m, :, c].astype(F32) + rc[m].astype(F32)).astype(BF16)
-        for n, way in enumerate(DIRS):
-            far = REACH[way] - step
-            if far < 1:
-                continue
-            source = qb.at[m, mod(z + way * far, 8)]
-            if step > 0:
-                s_copies[m, way, step - 1].arrived()
-                total = source[...].astype(F32) + rz[m, n, step - 1].astype(F32)
-                source = zs.at[m, n, step]
-                source[...] = total.astype(BF16)
-            s_copies[m, way, step] = Copy(source, rz.at[m, n, step], rz.at[m, n, step], at_z(way))
-
-    def sum_in(m):
-        s_copies[m, 1, 3].arrived()
-        s_copies[m, -1, 2].arrived()
-        total = qb[m, z].astype(F32) + rz[m, 0, 3].astype(F32) + rz[m, 1, 2].astype(F32)
+    FARTHEST_FIRST = (4, 3, 5, 2, 6, 1, 7)
+
+    def sum_out(m, first):
+        first.arrived()
+        qb[m] = (pb[m, :, c].astype(F32) + rc[m].astype(F32)).astype(BF16)
+        return [
+            Copy(qb.at[m, mod(z + k, 8)], rz.at[m, k], rz.at[m, k], at_z(k)) for k in FARTHEST_FIRST
+        ]
+
+    def sum_in(m, parts):
+        total = qb[m, z].astype(F32)
+        for k, copy in zip(FARTHEST_FIRST, parts):
+            copy.arrived()
+            total = total + rz[m, k].astype(F32)
         st[m] = total.astype(BF16)
 
     def norm_side(back_normed, scaled, reciprocal, cot):
@@ -298,12 +308,11 @@
         )
         return (cot.astype(F32) + back_state).astype(BF16)
 
-    hidden_side(0, acts[2].reshape(128, d))
+    hidden_side(0, acts[1].reshape(128, d))
     gain_term, first = back_side(0)
-    for step in range(4):
-        sum_step(0, step, first)
+    parts = sum_out(0, first)
     scaled, reciprocal = scaled_of(n_s[0], n_s[1])
-    sum_in(0)
+    sum_in(0, parts)
     hands = [
         Copy(st.at[0], nb.at[l], nb.at[l], before),
         Copy(st.at[0], nb.at[l], nb.at[1 - l], before_l),
@@ -311,9 +320,17 @@
     for copy in hands:
         copy.arrived()
     cots[z, c] = norm_side(nb[0].astype(F32) + nb[1].astype(F32), scaled, reciprocal, n_c[...])
-    r_copies, across = {}, []
-    for step in range(5):
-        ring_z(step, lambda row, core: cots.at[row, core], r_copies, across)
+
+    def cots_to_core(row):
+        return Copy(cots.at[row, c], cots.at[row, c], cots.at[row, 1 - c], pair_c)
+
+    spread = [
+        Copy(cots.at[z, c], cots.at[z, c], cots.at[mod(z - k, 8), c], at_z(k)) for k in FARTHEST_FIRST
+    ]
+    across = [cots_to_core(z)]
+    for k, copy in zip(FARTHEST_FIRST, spread):
+        copy.arrived()
+        across.append(cots_to_core(mod(z - k, 8)))
     for copy in across:
         copy.arrived()
 
@@ -377,44 +394,42 @@
     ga_step(0)
     ga_step(1)
     xc[:, :, 128:256] = turned(cots[...].reshape(128, d))
-    gx_step(4)
-    gx_step(3)
-    gx_step(-3)
+    for far in (4, 3, -3, 2, -2):
+        gx_step(far)
+    ga_step(2)
     term, first = back_side(1)
     ga[0] = (gain_term + term) * scale / gain_wide
     gain_c = Copy(ga.at[0], ga.at[1], ga.at[1], pair_c)
-    ga_step(2)
-    gx_step(2)
-    gx_step(-2)
+    for far in (1, -1, 0):
+        gx_step(far)
+    ga_step(3)
+    parts = sum_out(1, first)
+    gain_c.arrived()
+    ga[2 + 2 * h + l] = ga[0] + ga[1]
+    mine = ga.at[2 + 2 * h + l]
+    gain_x = [
+        Copy(mine, mine, ga.at[2 + 2 * h + 1 - l], pair_l),
+        Copy(mine, mine, ga.at[2 + 2 * g + l], pair_h),
+        Copy(mine, mine, ga.at[2 + 2 * g + 1 - l], pair_hl),
+    ]
     gb_step(4)
-    sum_step(1, 0, first)
-    gx_step(1)
-    gx_step(-1)
-    gx_step(0)
-    ga_step(3)
-    sum_step(1, 1, first)
-    gain_c.arrived()
-    ga[2] = ga[0] + ga[1]
-    gain_l = Copy(ga.at[2], ga.at[3], ga.at[3], pair_l)
+    ga_step(4)
+    for copy in gain_x:
+        copy.arrived()
+    gz[z] = (ga[2] + ga[3]) + (ga[4] + ga[5])
+    gain_z = [Copy(gz.at[z], gz.at[z], gz.at[mod(z - k, 8)], at_z(k)) for k in FARTHEST_FIRST]
     gb_step(3)
-    sum_step(1, 2, first)
-    gain_l.arrived()
-    ga[4] = ga[2] + ga[3]
-    gain_h = Copy(ga.at[4], ga.at[5], ga.at[5], pair_h)
-    ga_step(4)
-    sum_step(1, 3, first)
-    gain_h.arrived()
-    gz[z] = ga[4] + ga[5]
-    gain_z = [Copy(gz.at[z], gz.at[z], gz.at[mod(z - k, 8)], at_z(k)) for k in range(1, 8)]
-    gb_step(2)
-    sum_in(1)
-    last = Copy(st.at[1], sr, sr, pair_l)
     ga_step(5)
     for copy in gain_z:
         copy.arrived()
     gy[y] = jnp.sum(gz[...], axis=0)
-    gain_y = [Copy(gy.at[y], gy.at[y], gy.at[mod(y - k, 8)], at_y(k)) for k in range(1, 8)]
+    gain_y = [Copy(gy.at[y], gy.at[y], gy.at[mod(y - k, 8)], at_y(k)) for k in FARTHEST_FIRST]
     ga_step(6)
+    sum_in(1, parts)
+    last = Copy(st.at[1], sr, sr, pair_l)
+    gb_step(2)
+    fs[...] = ga_end(1).astype(BF16)
+    final = Copy(fs, fr, fr, pair_h)
     gb_step(1)
     scaled, reciprocal = scaled_of(e_s[0, 1], e_s[1, 1])
     last.arrived()
@@ -423,11 +438,7 @@
     for copy in gain_y:
         copy.arrived()
     gain_out[...] = jnp.sum(gy[...], axis=0).reshape(d)
-
-    fs[...] = ga_end(1).astype(BF16)
-    final = Copy(fs, fr, fr, pair_h)
     up_main = ga_end(0)
-    down_main, fold = None, None
     pair = b_pair(0)
     for j in (0, 1):
         for n, way in enumerate(DIRS):
@@ -456,7 +467,7 @@
         e_s=(2, 2, 4, d), e_c=(2, 4, d), n_s=(2, 4, d), n_c=(8, d), nb=(2, 8, d),
         acts=(3, 8, 2, 8, d), cots=(8, 2, 8, d), xn=(16, rows, 256), xc=(16, rows, 256),
         bm=(256, 256), hm=(256, 256), br=(256, 128), hr=(256, 128),
-        pb=(2, 8, 2, 8, d), rc=(2, 8, 8, d), qb=(2, 8, 8, d), zs=(2, 2, 4, 8, d), rz=(2, 2, 4, 8, d),
+        pb=(2, 8, 2, 8, d), rc=(2, 8, 8, d), qb=(2, 8, 8, d), rz=(2, 8, 8, d),
         st=(2, 8, d), sr=(8, d),
         gas=(2, 7, rows, 256), gar=(2, 7, rows, 256),
         gx0=(8, rows + 88, 128), gx1=(8, rows, 128), hx0=(8, rows + 88, 128), hx1=(8, rows, 128),

time: 132 us -> 121 us (0.917)
  the two profiles are of different devices: /device:TPU:6 before, /device:TPU:8 now
where the time goes in v3:
time: 121 us
  Pallas kernels  115 us (95%)
  local copies, waits for them, and re-layouts  4.26 us (4%)
  between operations  1.29 us (1%)
    pallas_call x1, Pallas kernels, on_device(): pl.pallas_call(functools.partial(kernel, scale), out_shape=(jax.ShapeDtyp...  115 us
    unnamed x8, local copies, waits for them, and re-layouts  4.26 us

profile of v3, /device:TPU:8, one launch (start us, length us, event | category | flops | bytes accessed | tf_op | source)
XLA Modules:
  0.0 121.0 jit_solution(15536150404387132954)
XLA Ops:
  1.3 115.4 %shard_map.93 = (bf16[1,4,2688]{2,1,0:T(4,128)(2,1)}, bf16[168,288]{1,0:T(8,128)(2,1)}, bf16[168,288]{1,0:T(8,128)(2,1)}, f32[2688]{0:T(1024)}) custom-call(bf16[1,2,4,2688]{3,2,1,0:T(4,128)(2,1)} %states.1, bf16[1,4,2688]{2,1,0:T(4,128)(2,1)} %cot_in.1, s32[1]{0:T(128)S(6)} %copy.14.lengths, bf16[2688]{0:T(1024)(128)(2,1)} %gain.1, bf16[168,288]{1,0:T(8,128)(2,1)} %up.1, ...), custom_call_target="tpu_custom_call" | custom-call | tf_op jit(solution)/shard_map/pallas_call | solution.py:478
  116.7 1.3 %copy.15 = bf16[1,4,2688]{2,1,0:T(4,128)(2,1)} copy(bf16[1,4,2688]{2,1,0:T(4,128)(2,1)} %get-tuple-element.16) | data formatting | bytes 43008
  118.0 0.0 copy-start
  118.0 1.6 %copy.16 = bf16[168,288]{1,0:T(8,128)(2,1)} copy(bf16[168,288]{1,0:T(8,128)(2,1)} %get-tuple-element.17) | data formatting | bytes 193536
  119.7 0.0 copy-done
  119.7 0.0 copy-start.1
  119.7 0.7 copy.17
  120.3 0.1 copy-done.1
  120.4 0.6 copy.18
Async XLA Ops:
  118.0 1.6 %copy-start = (bf16[168,288]{1,0:T(8,128)(2,1)S(1)}, bf16[168,288]{1,0:T(8,128)(2,1)}, u32[]{:S(2)}) copy-start(bf16[168,288]{1,0:T(8,128)(2,1)} %get-tuple-element.10) | copy-start | bytes 290308
  119.7 0.7 copy-start.1

commit v4 on v3

--- a/solution.py
+++ b/solution.py
@@ -214,15 +214,15 @@
         return value.astype(F32).T.astype(BF16).reshape(16, rows, 128)
 
     z_near(FIRST)
+    a_step(1)
     z_near(SECOND)
     a_step(2)
-    a_step(1)
     next_s = Copy(e_s.at[:, 0], n_s, n_s, before)
     next_c = Copy(acts.at[1, z, c], n_c, n_c, before)
     b_step(2)
+    a_step(3)
+    z_far(FIRST)
     a_step(4)
-    z_far(FIRST)
-    a_step(3)
     b_step(3)
     a_step(5)
     z_far(SECOND)
@@ -403,41 +403,42 @@
     for far in (1, -1, 0):
         gx_step(far)
     ga_step(3)
+    gain_c.arrived()
+    gz[z] = ga[0] + ga[1]
+    gain_z = [Copy(gz.at[z], gz.at[z], gz.at[mod(z - k, 8)], at_z(k)) for k in FARTHEST_FIRST]
     parts = sum_out(1, first)
-    gain_c.arrived()
-    ga[2 + 2 * h + l] = ga[0] + ga[1]
+    gb_step(4)
+    ga_step(4)
+    gb_step(3)
+    for copy in gain_z:
+        copy.arrived()
+    gy[y] = jnp.sum(gz[...], axis=0)
+    gain_y = [Copy(gy.at[y], gy.at[y], gy.at[mod(y - k, 8)], at_y(k)) for k in FARTHEST_FIRST]
+    ga_step(5)
+    ga_step(6)
+    gb_step(2)
+    sum_in(1, parts)
+    last = Copy(st.at[1], sr, sr, pair_l)
+    fs[...] = ga_end(1).astype(BF16)
+    final = Copy(fs, fr, fr, pair_h)
+    for copy in gain_y:
+        copy.arrived()
     mine = ga.at[2 + 2 * h + l]
+    mine[...] = jnp.sum(gy[...], axis=0)
     gain_x = [
         Copy(mine, mine, ga.at[2 + 2 * h + 1 - l], pair_l),
         Copy(mine, mine, ga.at[2 + 2 * g + l], pair_h),
         Copy(mine, mine, ga.at[2 + 2 * g + 1 - l], pair_hl),
     ]
-    gb_step(4)
-    ga_step(4)
-    for copy in gain_x:
-        copy.arrived()
-    gz[z] = (ga[2] + ga[3]) + (ga[4] + ga[5])
-    gain_z = [Copy(gz.at[z], gz.at[z], gz.at[mod(z - k, 8)], at_z(k)) for k in FARTHEST_FIRST]
-    gb_step(3)
-    ga_step(5)
-    for copy in gain_z:
-        copy.arrived()
-    gy[y] = jnp.sum(gz[...], axis=0)
-    gain_y = [Copy(gy.at[y], gy.at[y], gy.at[mod(y - k, 8)], at_y(k)) for k in FARTHEST_FIRST]
-    ga_step(6)
-    sum_in(1, parts)
-    last = Copy(st.at[1], sr, sr, pair_l)
-    gb_step(2)
-    fs[...] = ga_end(1).astype(BF16)
-    final = Copy(fs, fr, fr, pair_h)
     gb_step(1)
     scaled, reciprocal = scaled_of(e_s[0, 1], e_s[1, 1])
     last.arrived()
     result = norm_side(st[1].astype(F32) + sr[...].astype(F32), scaled, reciprocal, cots[z, c])
     cot_out[0] = jnp.where(l == 0, result[0:4].astype(F32), result[4:8].astype(F32)).astype(BF16)
-    for copy in gain_y:
-        copy.arrived()
-    gain_out[...] = jnp.sum(gy[...], axis=0).reshape(d)
+    for copy in gain_x:
+        copy.arrived()
+    gain_out[...] = ((ga[2] + ga[3]) + (ga[4] + ga[5])).reshape(d)
+
     up_main = ga_end(0)
     pair = b_pair(0)
     for j in (0, 1):

time: 121 us -> 108 us (0.89)
  the two profiles are of different devices: /device:TPU:8 before, /device:TPU:6 now
where the time goes in v4:
time: 108 us
  Pallas kernels  102 us (94%)
  local copies, waits for them, and re-layouts  4.26 us (4%)
  between operations  1.29 us (1%)
    pallas_call x1, Pallas kernels, on_device(): pl.pallas_call(functools.partial(kernel, scale), out_shape=(jax.ShapeDtyp...  102 us
    unnamed x8, local copies, waits for them, and re-layouts  4.26 us

profile of v4, /device:TPU:6, one launch (start us, length us, event | category | flops | bytes accessed | tf_op | source)
XLA Modules:
  0.0 107.9 jit_solution(2993433841465011127)
XLA Ops:
  1.3 102.4 %shard_map.93 = (bf16[1,4,2688]{2,1,0:T(4,128)(2,1)}, bf16[168,288]{1,0:T(8,128)(2,1)}, bf16[168,288]{1,0:T(8,128)(2,1)}, f32[2688]{0:T(1024)}) custom-call(bf16[1,2,4,2688]{3,2,1,0:T(4,128)(2,1)} %states.1, bf16[1,4,2688]{2,1,0:T(4,128)(2,1)} %cot_in.1, s32[1]{0:T(128)S(6)} %copy.14.lengths, bf16[2688]{0:T(1024)(128)(2,1)} %gain.1, bf16[168,288]{1,0:T(8,128)(2,1)} %up.1, ...), custom_call_target="tpu_custom_call" | custom-call | tf_op jit(solution)/shard_map/pallas_call | solution.py:479
  103.7 1.3 %copy.15 = bf16[1,4,2688]{2,1,0:T(4,128)(2,1)} copy(bf16[1,4,2688]{2,1,0:T(4,128)(2,1)} %get-tuple-element.16) | data formatting | bytes 43008
  105.0 0.0 copy-start
  105.0 1.6 %copy.16 = bf16[168,288]{1,0:T(8,128)(2,1)} copy(bf16[168,288]{1,0:T(8,128)(2,1)} %get-tuple-element.17) | data formatting | bytes 193536
  106.6 0.0 copy-done
  106.6 0.0 copy-start.1
  106.6 0.7 copy.17
  107.3 0.1 copy-done.1
  107.3 0.6 copy.18
Async XLA Ops:
  105.0 1.6 %copy-start = (bf16[168,288]{1,0:T(8,128)(2,1)S(1)}, bf16[168,288]{1,0:T(8,128)(2,1)}, u32[]{:S(2)}) copy-start(bf16[168,288]{1,0:T(8,128)(2,1)} %get-tuple-element.10) | copy-start | bytes 290308
  106.6 0.7 copy-start.1

commit v5 on v4

--- a/solution.py
+++ b/solution.py
@@ -21,7 +21,7 @@
     -1: ((1, 4), (0, 3), (1, 3), (0, 2), (1, 2), (0, 1), (1, 1)),
 }
 DIRS = (1, -1)
-N_COPIES = 176
+N_OUT, N_ARRIVALS = 102, 153
 
 
 def mod(a, n):
@@ -45,12 +45,12 @@
 
 
 def kernel(
-    scale, states, cot_in, lengths, gain, up, down,
+    scale, states_in, cot_in, lengths, gain_in, up_in, down_in,
     cot_out, up_out, down_out, gain_out,
     wa, wb0, wb1, wr, e_s, e_c, n_s, n_c, nb, acts, cots, xn, xc, bm, hm, br, hr,
     pb, rc, qb, rz, st, sr,
     gas, gar, gx0, gx1, hx0, hx1, gs0, gs1, gr0, gr1, fs, fr,
-    ga, gz, gy, send, recv,
+    gain, up, down, slope, ga, gz, gy, send, recv, local,
 ):
     s, p = lax.axis_index("section"), lax.axis_index("dp")
     y, h = lax.div(s, 2), lax.rem(s, 2)
@@ -78,22 +78,38 @@
 
     pending = []
 
+    arrivals, flushed, most = [0], [0], [0]
+
+    def flush():
+        for copy in pending[flushed[0] :]:
+            copy.out.wait_send()
+        most[0] = max(most[0], len(pending) - flushed[0])
+        flushed[0] = len(pending)
+
+    def new_arrival():
+        arrivals[0] += 1
+        return arrivals[0] - 1
+
     class Copy:
-        def __init__(self, src, dst, landing, device):
-            k = len(pending)
+        def __init__(self, src, dst, landing, device, group=None):
+            n = len(pending) - flushed[0]
+            k = new_arrival() if group is None else group
             self.out = pltpu.make_async_remote_copy(
-                src_ref=src, dst_ref=dst, send_sem=send.at[k], recv_sem=recv.at[k],
+                src_ref=src, dst_ref=dst, send_sem=send.at[n], recv_sem=recv.at[k],
                 device_id=device, device_id_type=MESH,
             )
-            self.arrival = pltpu.make_async_remote_copy(
-                src_ref=src, dst_ref=landing, send_sem=send.at[k], recv_sem=recv.at[k],
-                device_id=device, device_id_type=MESH,
-            )
+            self.landing, self.k = landing, k
             pending.append(self)
             self.out.start()
 
         def arrived(self):
-            self.arrival.wait_recv()
+            all_arrived(self.k, self.landing)
+
+    def all_arrived(group, landing):
+        pltpu.make_async_remote_copy(
+            src_ref=landing, dst_ref=landing, send_sem=send.at[0], recv_sem=recv.at[group],
+            device_id=pair_c, device_id_type=MESH,
+        ).wait_recv()
 
     barrier = pltpu.get_barrier_semaphore()
     partners = [at_y(k) for k in range(1, 8)] + [at_z(k) for k in range(1, 8)]
@@ -102,8 +118,23 @@
     for device in partners:
         pl.semaphore_signal(barrier, inc=1, device_id=device, device_id_type=MESH)
 
+    own = [
+        pltpu.make_async_copy(source, target, local.at[k])
+        for k, (source, target) in enumerate(
+            (
+                (up_in, up), (down_in, down), (states_in.at[0], e_s.at[l]),
+                (cot_in.at[0], e_c.at[l]), (gain_in, gain),
+            )
+        )
+    ]
+    for copy in own:
+        copy.start()
+    for copy in own:
+        copy.wait()
+
     rows = up.shape[0]
-    wa[y, h] = up[:, 0:256]
+    for j in (0, 1):
+        wa[j, y, h] = up[:, 128 * j : 128 * (j + 1)]
     wb0[y, h, 0:rows, :] = down[:, 0:128]
     wb1[y, h] = down[:, 128:256]
     wb0[y, h, rows : rows + 88, :] = folded(
@@ -112,30 +143,31 @@
             axis=1,
         )
     ).astype(BF16)
-    e_s[l] = states[0]
-    e_c[l] = cot_in[0]
 
     pl.semaphore_wait(barrier, len(partners))
 
     swap_s = Copy(e_s.at[l], e_s.at[l], e_s.at[1 - l], pair_l)
     swap_c = Copy(e_c.at[l], e_c.at[l], e_c.at[1 - l], pair_l)
-    swap_w = Copy(wa.at[y, h], wa.at[y, h], wa.at[y, g], pair_h)
-    a_copies, b_copies, x_copies = {}, {}, []
+    swap_w = [Copy(wa.at[j, y, h], wa.at[j, y, h], wa.at[j, y, g], pair_h) for j in (0, 1)]
+    a_copies, b_copies = {}, {}
+    x_group = [new_arrival(), new_arrival()]
 
     def a_step(i):
-        for way in DIRS:
-            sub, far = A_ITEMS[way][i]
-            if far > 0:
-                a_copies[way, sub, far - 1].arrived()
-            elif sub == 1 and way == 1:
-                swap_w.arrived()
-            row = mod(y - way * far, 8)
-            land = mod(y - way * (far + 1), 8)
-            at_h = g if sub else h
-            a_copies[way, sub, far] = Copy(wa.at[row, at_h], wa.at[row, at_h], wa.at[land, at_h], at_y(way))
+        for j in (0, 1):
+            for way in DIRS:
+                sub, far = A_ITEMS[way][i]
+                if far > 0:
+                    a_copies[way, sub, far - 1, j].arrived()
+                elif sub == 1 and way == 1:
+                    swap_w[j].arrived()
+                row = mod(y - way * far, 8)
+                land = mod(y - way * (far + 1), 8)
+                at_h = g if sub else h
+                block = wa.at[j, row, at_h]
+                a_copies[way, sub, far, j] = Copy(block, block, wa.at[j, land, at_h], at_y(way))
 
     def b_across(row, j):
-        x_copies.append(Copy(wb[j].at[row, h], wb[j].at[row, h], wb[j].at[row, g], pair_h))
+        Copy(wb[j].at[row, h], wb[j].at[row, h], None, pair_h, x_group[j])
 
     def b_step(far):
         for way in DIRS:
@@ -176,7 +208,7 @@
     acts[1, z, c] = jnp.where(position < lengths[0], raw, 0.0).astype(BF16)
 
     FIRST, SECOND = slice(0, 2), slice(2, 3)
-    z_copies, c_copies = {}, []
+    z_copies, c_group = {}, new_arrival()
 
     def act(part, row, core):
         return acts.at[part, row, core]
@@ -187,7 +219,7 @@
 
     def z_core(part, row):
         row = mod(row, 8)
-        c_copies.append(Copy(act(part, row, c), act(part, row, c), act(part, row, 1 - c), pair_c))
+        Copy(act(part, row, c), act(part, row, c), None, pair_c, c_group)
 
     def z_near(part):
         for k in (2, -2, 1, -1):
@@ -216,22 +248,21 @@
     z_near(FIRST)
     a_step(1)
     z_near(SECOND)
+    b_step(2)
     a_step(2)
+    a_step(3)
+    b_step(3)
+    z_far(FIRST)
+    a_step(4)
+    b_step(4)
+    a_step(5)
+    z_far(SECOND)
     next_s = Copy(e_s.at[:, 0], n_s, n_s, before)
     next_c = Copy(acts.at[1, z, c], n_c, n_c, before)
-    b_step(2)
-    a_step(3)
-    z_far(FIRST)
-    a_step(4)
-    b_step(3)
-    a_step(5)
-    z_far(SECOND)
-    b_step(4)
     a_step(6)
     z_last(FIRST)
     z_last(SECOND)
-    for copy in c_copies:
-        copy.arrived()
+    all_arrived(c_group, acts.at[:, pl.ds(0, 4)])
     xn[:, :, 0:128] = turned(acts[0].reshape(128, d))
     xn[:, :, 128:256] = turned(acts[2].reshape(128, d))
     xc[:, :, 0:128] = turned(acts[1].reshape(128, d))
@@ -240,66 +271,82 @@
     for way in DIRS:
         for sub in (0, 1):
             last = max(f for q, f in A_ITEMS[way] if q == sub)
-            a_copies[way, sub, last].arrived()
-    for copy in x_copies:
-        copy.arrived()
+            for j in (0, 1):
+                a_copies[way, sub, last, j].arrived()
+    for j in (0, 1):
+        all_arrived(x_group[j], wb[j].at[pl.ds(0, 4)])
     for row in range(8):
         for k in range(2):
             fold = wb0[row, k, rows : rows + 88, :].astype(F32)
             wr[row, k] = jnp.concatenate([fold, pltpu.roll(fold[0:80], 64, 1)], axis=0).astype(BF16)
 
+    flush()
     lane = lax.broadcasted_iota(jnp.int32, (128, 128), 1)
 
-    def gate(hidden, back):
-        sigma = jax.nn.sigmoid(hidden)
-        return hidden * sigma, back * sigma * (1.0 + hidden * (1.0 - sigma))
+    def up_main():
+        return jnp.concatenate([wa[0].reshape(d, 128), wa[1].reshape(d, 128)], axis=1)
+
+    def forward_side(m):
+        normed = acts[2 * m].reshape(128, d)
+        hidden, hidden_rest = dot(normed, up_main()), dot(normed, wr[...].reshape(d, 128))
+        sigma, sigma_rest = jax.nn.sigmoid(hidden), jax.nn.sigmoid(hidden_rest)
+        at_m = slice(128 * m, 128 * (m + 1))
+        hm[at_m, :] = (hidden * sigma).astype(BF16)
+        rest_out = jnp.where(lane < 32, hidden_rest * sigma_rest, 0.0)
+        hr[at_m, :] = pltpu.roll(rest_out, 32, 1).astype(BF16)
+        slope[m, :, 0:256] = sigma * (1.0 + hidden * (1.0 - sigma))
+        slope[m, :, 256:384] = sigma_rest * (1.0 + hidden_rest * (1.0 - sigma_rest))
 
     def hidden_side(m, cot):
-        normed = acts[2 * m].reshape(128, d)
         down_main = jnp.concatenate(
             [wb0[:, :, 0:rows, :].reshape(d, 128), wb1[...].reshape(d, 128)], axis=1
         )
-        hidden_out, back_in = gate(dot(normed, wa[...].reshape(d, 256)), dot(cot, down_main))
-        rest = wr[...].reshape(d, 128)
-        rest_out, rest_in = gate(dot(normed, rest), pltpu.roll(dot(cot, rest), 96, 1))
-        rest_out = jnp.where(lane < 32, rest_out, 0.0)
-        rest_in = jnp.where(lane < 32, rest_in, 0.0)
         at_m = slice(128 * m, 128 * (m + 1))
-        bm[at_m, :] = back_in.astype(BF16)
-        br[at_m, :] = rest_in.astype(BF16)
-        hm[at_m, :] = hidden_out.astype(BF16)
-        hr[at_m, :] = pltpu.roll(rest_out, 32, 1).astype(BF16)
+        bm[at_m, :] = (dot(cot, down_main) * slope[m, :, 0:256]).astype(BF16)
+        rest_in = pltpu.roll(dot(cot, wr[...].reshape(d, 128)), 96, 1) * slope[m, :, 256:384]
+        br[at_m, :] = jnp.where(lane < 32, rest_in, 0.0).astype(BF16)
+
+    PIECES = [(k, 896) for k in range(0, d, 896)]
+    FARTHEST_FIRST = (4, 3, 5, 2, 6, 1, 7)
 
     def back_side(m):
-        normed = acts[2 * m].reshape(128, d)
         at_m = slice(128 * m, 128 * (m + 1))
         back_in, rest_in = bm[at_m, :], br[at_m, :]
-        wide, rest = wa[...].reshape(d, 256), wr[...].reshape(d, 128)
-        term = []
-        step = 896
-        for k in range(0, d, step):
-            partial = dot_t(back_in, wide[k : k + step]) + dot_t(rest_in, rest[k : k + step])
-            pb[m, :, :, :, k : k + step] = partial.astype(BF16).reshape(8, 2, 8, step)
+        wide, rest = up_main(), wr[...].reshape(d, 128)
+        normed = acts[2 * m].reshape(128, d)
+        term, first = [], []
+        for k, n in PIECES:
+            partial = dot_t(back_in, wide[k : k + n]) + dot_t(rest_in, rest[k : k + n])
+            pb[m, :, :, :, k : k + n] = partial.astype(BF16).reshape(8, 2, 8, n)
+            cut = (m, slice(None), slice(None), pl.ds(k, n))
+            first.append(
+                Copy(pb.at[m, :, 1 - c, :, pl.ds(k, n)], rc.at[cut], rc.at[cut], pair_c)
+            )
             term.append(
-                jnp.sum(partial * normed[:, k : k + step].astype(F32), axis=0, keepdims=True)
+                jnp.sum(partial * normed[:, k : k + n].astype(F32), axis=0, keepdims=True)
             )
-        return jnp.concatenate(term, axis=1), Copy(pb.at[m, :, 1 - c], rc.at[m], rc.at[m], pair_c)
-
-    FARTHEST_FIRST = (4, 3, 5, 2, 6, 1, 7)
+        return jnp.concatenate(term, axis=1), first
 
     def sum_out(m, first):
-        first.arrived()
-        qb[m] = (pb[m, :, c].astype(F32) + rc[m].astype(F32)).astype(BF16)
-        return [
-            Copy(qb.at[m, mod(z + k, 8)], rz.at[m, k], rz.at[m, k], at_z(k)) for k in FARTHEST_FIRST
-        ]
-
-    def sum_in(m, parts):
-        total = qb[m, z].astype(F32)
-        for k, copy in zip(FARTHEST_FIRST, parts):
+        groups = []
+        for (k, n), copy in zip(PIECES, first):
             copy.arrived()
-            total = total + rz[m, k].astype(F32)
-        st[m] = total.astype(BF16)
+            qb[m, :, :, k : k + n] = (
+                pb[m, :, c, :, k : k + n].astype(F32) + rc[m, :, :, k : k + n].astype(F32)
+            ).astype(BF16)
+            groups.append(new_arrival())
+            for far in FARTHEST_FIRST:
+                source, land = qb.at[m, mod(z + far, 8), :, pl.ds(k, n)], rz.at[m, far, :, pl.ds(k, n)]
+                Copy(source, land, None, at_z(far), groups[-1])
+        return groups
+
+    def sum_in(m, groups):
+        for (k, n), group in zip(PIECES, groups):
+            all_arrived(group, rz.at[m, pl.ds(1, 7), :, pl.ds(k, n)])
+            total = qb[m, z, :, k : k + n].astype(F32)
+            for far in FARTHEST_FIRST:
+                total = total + rz[m, far, :, k : k + n].astype(F32)
+            st[m, :, k : k + n] = total.astype(BF16)
 
     def norm_side(back_normed, scaled, reciprocal, cot):
         gained = back_normed * gain_wide
@@ -308,9 +355,11 @@
         )
         return (cot.astype(F32) + back_state).astype(BF16)
 
+    forward_side(0)
     hidden_side(0, acts[1].reshape(128, d))
     gain_term, first = back_side(0)
     parts = sum_out(0, first)
+    forward_side(1)
     scaled, reciprocal = scaled_of(n_s[0], n_s[1])
     sum_in(0, parts)
     hands = [
@@ -321,39 +370,52 @@
         copy.arrived()
     cots[z, c] = norm_side(nb[0].astype(F32) + nb[1].astype(F32), scaled, reciprocal, n_c[...])
 
+    across = new_arrival()
+
     def cots_to_core(row):
-        return Copy(cots.at[row, c], cots.at[row, c], cots.at[row, 1 - c], pair_c)
+        Copy(cots.at[row, c], cots.at[row, c], None, pair_c, across)
 
     spread = [
         Copy(cots.at[z, c], cots.at[z, c], cots.at[mod(z - k, 8), c], at_z(k)) for k in FARTHEST_FIRST
     ]
-    across = [cots_to_core(z)]
+    cots_to_core(z)
     for k, copy in zip(FARTHEST_FIRST, spread):
         copy.arrived()
-        across.append(cots_to_core(mod(z - k, 8)))
-    for copy in across:
-        copy.arrived()
+        cots_to_core(mod(z - k, 8))
+    all_arrived(across, cots.at[pl.ds(0, 4)])
+
+    flush()
 
     hidden_side(1, cots[...].reshape(128, d))
     ga_copies, gx_copies, gb_copies = {}, {}, {}
 
     def ga_step(i):
-        for n, way in enumerate(DIRS):
+        values = []
+        for way in DIRS:
             sub, far = GA_ITEMS[way][i]
-            value = dot(xn[mod(y + way * far, 8) * 2 + (g if sub else h)], bm[...]) * scale
-            if (way, sub, far + 1) in ga_copies:
-                k = GA_ITEMS[way].index((sub, far + 1))
-                ga_copies[way, sub, far + 1].arrived()
-                value = value + gar[n, k].astype(F32)
-            gas[n, i] = value.astype(BF16)
-            ga_copies[way, sub, far] = Copy(gas.at[n, i], gar.at[n, i], gar.at[n, i], at_y(way))
+            values.append(dot(xn[mod(y + way * far, 8) * 2 + (g if sub else h)], bm[...]) * scale)
+        for j in (0, 1):
+            for n, way in enumerate(DIRS):
+                sub, far = GA_ITEMS[way][i]
+                value = values[n][:, 128 * j : 128 * (j + 1)]
+                if (way, sub, far + 1, j) in ga_copies:
+                    k = GA_ITEMS[way].index((sub, far + 1))
+                    ga_copies[way, sub, far + 1, j].arrived()
+                    value = value + gar[n, k, j].astype(F32)
+                gas[n, i, j] = value.astype(BF16)
+                land = gar.at[n, i, j]
+                ga_copies[way, sub, far, j] = Copy(gas.at[n, i, j], land, land, at_y(way))
 
     def ga_end(sub):
         value = dot(xn[y * 2 + (g if sub else h)], bm[...]) * scale
-        for n, way in enumerate(DIRS):
-            ga_copies[way, sub, 1].arrived()
-            value = value + gar[n, GA_ITEMS[way].index((sub, 1))].astype(F32)
-        return value
+        pieces = []
+        for j in (0, 1):
+            piece = value[:, 128 * j : 128 * (j + 1)]
+            for n, way in enumerate(DIRS):
+                ga_copies[way, sub, 1, j].arrived()
+                piece = piece + gar[n, GA_ITEMS[way].index((sub, 1)), j].astype(F32)
+            pieces.append(piece)
+        return jnp.concatenate(pieces, axis=1)
 
     def b_terms(far, at_h):
         k = mod(y + far, 8) * 2 + at_h
@@ -392,9 +454,10 @@
                 )
 
     ga_step(0)
+    xc[:, :, 128:256] = turned(cots[...].reshape(128, d))
+    gx_step(4)
     ga_step(1)
-    xc[:, :, 128:256] = turned(cots[...].reshape(128, d))
-    for far in (4, 3, -3, 2, -2):
+    for far in (3, -3, 2, -2):
         gx_step(far)
     ga_step(2)
     term, first = back_side(1)
@@ -405,15 +468,18 @@
     ga_step(3)
     gain_c.arrived()
     gz[z] = ga[0] + ga[1]
-    gain_z = [Copy(gz.at[z], gz.at[z], gz.at[mod(z - k, 8)], at_z(k)) for k in FARTHEST_FIRST]
+    gain_z = new_arrival()
+    for k in FARTHEST_FIRST:
+        Copy(gz.at[z], gz.at[z], None, at_z(k), gain_z)
     parts = sum_out(1, first)
     gb_step(4)
     ga_step(4)
     gb_step(3)
-    for copy in gain_z:
-        copy.arrived()
+    all_arrived(gain_z, gz.at[pl.ds(0, 7)])
     gy[y] = jnp.sum(gz[...], axis=0)
-    gain_y = [Copy(gy.at[y], gy.at[y], gy.at[mod(y - k, 8)], at_y(k)) for k in FARTHEST_FIRST]
+    gain_y = new_arrival()
+    for k in FARTHEST_FIRST:
+        Copy(gy.at[y], gy.at[y], None, at_y(k), gain_y)
     ga_step(5)
     ga_step(6)
     gb_step(2)
@@ -421,8 +487,7 @@
     last = Copy(st.at[1], sr, sr, pair_l)
     fs[...] = ga_end(1).astype(BF16)
     final = Copy(fs, fr, fr, pair_h)
-    for copy in gain_y:
-        copy.arrived()
+    all_arrived(gain_y, gy.at[pl.ds(0, 7)])
     mine = ga.at[2 + 2 * h + l]
     mine[...] = jnp.sum(gy[...], axis=0)
     gain_x = [
@@ -439,7 +504,7 @@
         copy.arrived()
     gain_out[...] = ((ga[2] + ga[3]) + (ga[4] + ga[5])).reshape(d)
 
-    up_main = ga_end(0)
+    up_sum = ga_end(0)
     pair = b_pair(0)
     for j in (0, 1):
         for n, way in enumerate(DIRS):
@@ -452,25 +517,25 @@
     up_out[:, 256:288] = rest[:, 0:32].astype(BF16)
     down_out[:, 256:288] = rest[:, 32:64].astype(BF16)
     final.arrived()
-    up_out[:, 0:256] = (up_main + fr[...].astype(F32)).astype(BF16)
-
-    assert len(pending) == N_COPIES, len(pending)
-    for copy in pending:
-        copy.out.wait_send()
+    up_out[:, 0:256] = (up_sum + fr[...].astype(F32)).astype(BF16)
+
+    flush()
+    assert (most[0], arrivals[0]) == (N_OUT, N_ARRIVALS), (most, arrivals)
 
 
 def on_device(scale, saved_states, cotangent_in, lengths, gain, up_weight, down_weight):
     d = gain.shape[0]
     rows, cols = up_weight.shape
     vmem = pl.BlockSpec(memory_space=pltpu.VMEM)
+    there = pl.BlockSpec(memory_space=pl.ANY)
     scratch = dict(
-        wa=(8, 2, rows, 256), wb0=(8, 2, rows + 88, 128), wb1=(8, 2, rows, 128), wr=(8, 2, rows, 128),
+        wa=(2, 8, 2, rows, 128), wb0=(8, 2, rows + 88, 128), wb1=(8, 2, rows, 128), wr=(8, 2, rows, 128),
         e_s=(2, 2, 4, d), e_c=(2, 4, d), n_s=(2, 4, d), n_c=(8, d), nb=(2, 8, d),
         acts=(3, 8, 2, 8, d), cots=(8, 2, 8, d), xn=(16, rows, 256), xc=(16, rows, 256),
         bm=(256, 256), hm=(256, 256), br=(256, 128), hr=(256, 128),
         pb=(2, 8, 2, 8, d), rc=(2, 8, 8, d), qb=(2, 8, 8, d), rz=(2, 8, 8, d),
         st=(2, 8, d), sr=(8, d),
-        gas=(2, 7, rows, 256), gar=(2, 7, rows, 256),
+        gas=(2, 7, 2, rows, 128), gar=(2, 7, 2, rows, 128),
         gx0=(8, rows + 88, 128), gx1=(8, rows, 128), hx0=(8, rows + 88, 128), hx1=(8, rows, 128),
         gs0=(2, 5, rows + 88, 128), gs1=(2, 5, rows, 128),
         gr0=(2, 5, rows + 88, 128), gr1=(2, 5, rows, 128),
@@ -484,11 +549,14 @@
             jax.ShapeDtypeStruct((rows, cols), BF16),
             jax.ShapeDtypeStruct((d,), F32),
         ),
-        in_specs=[vmem, vmem, pl.BlockSpec(memory_space=pltpu.SMEM), vmem, vmem, vmem],
+        in_specs=[there, there, pl.BlockSpec(memory_space=pltpu.SMEM), there, there, there],
         out_specs=(vmem,) * 4,
         scratch_shapes=[pltpu.VMEM(shape, BF16) for shape in scratch.values()]
+        + [pltpu.VMEM((d,), BF16)]
+        + [pltpu.VMEM((rows, cols), BF16)] * 2
+        + [pltpu.VMEM((2, 128, 384), F32)]
         + [pltpu.VMEM((n, 1, d), F32) for n in (6, 8, 8)]
-        + [pltpu.SemaphoreType.DMA((N_COPIES,))] * 2,
+        + [pltpu.SemaphoreType.DMA((n,)) for n in (N_OUT, N_ARRIVALS, 5)],
         compiler_params=pltpu.CompilerParams(
             collective_id=0, has_side_effects=True, vmem_limit_bytes=56 * 2**20
         ),

time: 108 us -> 107 us (level)
    pallas_call x1, Pallas kernels: 102 us -> 101 us  [on_device(): pl.pallas_call(functools.partial(kernel, scale), out_shape=(jax.ShapeDtyp...]
where the time goes in v5:
time: 107 us; the launch traced here: 106 us
  Pallas kernels  101 us (94%)
  local copies, waits for them, and re-layouts  4.26 us (4%)
  between operations  1.29 us (1%)
    pallas_call x1, Pallas kernels, on_device(): pl.pallas_call(functools.partial(kernel, scale), out_shape=(jax.ShapeDtyp...  101 us
    unnamed x8, local copies, waits for them, and re-layouts  4.26 us

profile of v5, /device:TPU:6, one launch (start us, length us, event | category | flops | bytes accessed | tf_op | source)
XLA Modules:
  0.0 106.2 jit_solution(6845849239134981519)
XLA Ops:
  1.3 100.7 %shard_map.93 = (bf16[1,4,2688]{2,1,0:T(4,128)(2,1)}, bf16[168,288]{1,0:T(8,128)(2,1)}, bf16[168,288]{1,0:T(8,128)(2,1)}, f32[2688]{0:T(1024)}) custom-call(bf16[1,2,4,2688]{3,2,1,0:T(4,128)(2,1)} %states_in.1, bf16[1,4,2688]{2,1,0:T(4,128)(2,1)} %cot_in.1, s32[1]{0:T(128)S(6)} %copy.14.lengths, bf16[2688]{0:T(1024)(128)(2,1)} %gain_in.1, ...), custom_call_target="tpu_custom_call" | custom-call | tf_op jit(solution)/shard_map/pallas_call | solution.py:544
  102.0 1.3 %copy.15 = bf16[1,4,2688]{2,1,0:T(4,128)(2,1)} copy(bf16[1,4,2688]{2,1,0:T(4,128)(2,1)} %get-tuple-element.16) | data formatting | bytes 43008
  103.3 0.0 copy-start
  103.3 1.6 %copy.16 = bf16[168,288]{1,0:T(8,128)(2,1)} copy(bf16[168,288]{1,0:T(8,128)(2,1)} %get-tuple-element.17) | data formatting | bytes 193536
  104.9 0.0 copy-done
  104.9 0.0 copy-start.1
  104.9 0.7 copy.17
  105.6 0.1 copy-done.1
  105.6 0.6 copy.18
Async XLA Ops:
  103.3 1.6 %copy-start = (bf16[168,288]{1,0:T(8,128)(2,1)S(1)}, bf16[168,288]{1,0:T(8,128)(2,1)}, u32[]{:S(2)}) copy-start(bf16[168,288]{1,0:T(8,128)(2,1)} %get-tuple-element.10) | copy-start | bytes 290308
  104.9 0.7 copy-start.1

commit v6 on v5

--- a/solution.py
+++ b/solution.py
@@ -263,9 +263,6 @@
     z_last(FIRST)
     z_last(SECOND)
     all_arrived(c_group, acts.at[:, pl.ds(0, 4)])
-    xn[:, :, 0:128] = turned(acts[0].reshape(128, d))
-    xn[:, :, 128:256] = turned(acts[2].reshape(128, d))
-    xc[:, :, 0:128] = turned(acts[1].reshape(128, d))
     next_s.arrived()
     next_c.arrived()
     for way in DIRS:
@@ -360,6 +357,9 @@
     gain_term, first = back_side(0)
     parts = sum_out(0, first)
     forward_side(1)
+    xn[:, :, 0:128] = turned(acts[0].reshape(128, d))
+    xn[:, :, 128:256] = turned(acts[2].reshape(128, d))
+    xc[:, :, 0:128] = turned(acts[1].reshape(128, d))
     scaled, reciprocal = scaled_of(n_s[0], n_s[1])
     sum_in(0, parts)
     hands = [
@@ -474,19 +474,17 @@
     parts = sum_out(1, first)
     gb_step(4)
     ga_step(4)
-    gb_step(3)
     all_arrived(gain_z, gz.at[pl.ds(0, 7)])
     gy[y] = jnp.sum(gz[...], axis=0)
     gain_y = new_arrival()
     for k in FARTHEST_FIRST:
         Copy(gy.at[y], gy.at[y], None, at_y(k), gain_y)
+    gb_step(3)
     ga_step(5)
     ga_step(6)
     gb_step(2)
     sum_in(1, parts)
     last = Copy(st.at[1], sr, sr, pair_l)
-    fs[...] = ga_end(1).astype(BF16)
-    final = Copy(fs, fr, fr, pair_h)
     all_arrived(gain_y, gy.at[pl.ds(0, 7)])
     mine = ga.at[2 + 2 * h + l]
     mine[...] = jnp.sum(gy[...], axis=0)
@@ -495,6 +493,8 @@
         Copy(mine, mine, ga.at[2 + 2 * g + l], pair_h),
         Copy(mine, mine, ga.at[2 + 2 * g + 1 - l], pair_hl),
     ]
+    fs[...] = ga_end(1).astype(BF16)
+    final = Copy(fs, fr, fr, pair_h)
     gb_step(1)
     scaled, reciprocal = scaled_of(e_s[0, 1], e_s[1, 1])
     last.arrived()

time: 107 us -> 107 us (level)
  no operation moved by 1% of the time
where the time goes in v6:
time: 107 us; the launch traced here: 106 us
  Pallas kernels  101 us (94%)
  local copies, waits for them, and re-layouts  4.26 us (4%)
  between operations  1.29 us (1%)
    pallas_call x1, Pallas kernels, on_device(): pl.pallas_call(functools.partial(kernel, scale), out_shape=(jax.ShapeDtyp...  101 us
    unnamed x8, local copies, waits for them, and re-layouts  4.26 us

profile of v6, /device:TPU:6, one launch (start us, length us, event | category | flops | bytes accessed | tf_op | source)
XLA Modules:
  0.0 106.4 jit_solution(12946286332588980958)
XLA Ops:
  1.3 100.8 %shard_map.93 = (bf16[1,4,2688]{2,1,0:T(4,128)(2,1)}, bf16[168,288]{1,0:T(8,128)(2,1)}, bf16[168,288]{1,0:T(8,128)(2,1)}, f32[2688]{0:T(1024)}) custom-call(bf16[1,2,4,2688]{3,2,1,0:T(4,128)(2,1)} %states_in.1, bf16[1,4,2688]{2,1,0:T(4,128)(2,1)} %cot_in.1, s32[1]{0:T(128)S(6)} %copy.14.lengths, bf16[2688]{0:T(1024)(128)(2,1)} %gain_in.1, ...), custom_call_target="tpu_custom_call" | custom-call | tf_op jit(solution)/shard_map/pallas_call | solution.py:544
  102.1 1.3 %copy.15 = bf16[1,4,2688]{2,1,0:T(4,128)(2,1)} copy(bf16[1,4,2688]{2,1,0:T(4,128)(2,1)} %get-tuple-element.16) | data formatting | bytes 43008
  103.4 0.0 copy-start
  103.4 1.6 %copy.16 = bf16[168,288]{1,0:T(8,128)(2,1)} copy(bf16[168,288]{1,0:T(8,128)(2,1)} %get-tuple-element.17) | data formatting | bytes 193536
  105.0 0.0 copy-done
  105.0 0.0 copy-start.1
  105.1 0.7 copy.17
  105.7 0.1 copy-done.1
  105.8 0.6 copy.18
Async XLA Ops:
  103.4 1.6 %copy-start = (bf16[168,288]{1,0:T(8,128)(2,1)S(1)}, bf16[168,288]{1,0:T(8,128)(2,1)}, u32[]{:S(2)}) copy-start(bf16[168,288]{1,0:T(8,128)(2,1)} %get-tuple-element.10) | copy-start | bytes 290308
  105.0 0.7 copy-start.1
